TPU v7x, 32 devices: a whole 2x2x4 slice. The times are simulated.
32 devices in a mesh: dp: 16 (over z, y, x), ffn: 2 (over core).
Axes of the slice: x: 2, y: 2, z: 4, core: 2. Of those that a mesh axis runs over, the one named last changes fastest.
Arguments:
- item_table: float32 [25088, 256], P(('dp', 'ffn')), may hold values from -0.75 to 0.75
- attn_in: float32 [3, 256, 512], P(None, None, 'ffn'), may hold values from -0.375 to 0.375
- attn_out: float32 [512, 256], P('ffn'), may hold values from -0.75 to 0.75
- ffn_up: float32 [256, 1024], P(None, 'ffn'), may hold values from -0.375 to 0.375
- ffn_down: float32 [1024, 256], P('ffn'), may hold values from -0.1875 to 0.1875
- position_table: float32 [512, 256], replicated, may hold values from -3 to 3
- norm_gains: float32 [3, 256], replicated, may hold values from 0.5 to 1.5
- item_first: float32 [25088, 256], P(('dp', 'ffn')), may hold values from -0.00015957387 to 0.00015957387
- item_second: float32 [25088, 256], P(('dp', 'ffn')), may hold values from 1.31528e-10 to 5.26112e-10
- attn_in_first: float32 [3, 256, 512], P(None, None, 'ffn'), may hold values from -0.00015957387 to 0.00015957387
- attn_in_second: float32 [3, 256, 512], P(None, None, 'ffn'), may hold values from 1.31528e-10 to 5.26112e-10
- attn_out_first: float32 [512, 256], P('ffn'), may hold values from -0.00015957387 to 0.00015957387
- attn_out_second: float32 [512, 256], P('ffn'), may hold values from 1.31528e-10 to 5.26112e-10
- ffn_up_first: float32 [256, 1024], P(None, 'ffn'), may hold values from -0.00015957387 to 0.00015957387
- ffn_up_second: float32 [256, 1024], P(None, 'ffn'), may hold values from 1.31528e-10 to 5.26112e-10
- ffn_down_first: float32 [1024, 256], P('ffn'), may hold values from -0.00015957387 to 0.00015957387
- ffn_down_second: float32 [1024, 256], P('ffn'), may hold values from 1.31528e-10 to 5.26112e-10
- position_first: float32 [512, 256], replicated, may hold values from -0.00015957387 to 0.00015957387
- position_second: float32 [512, 256], replicated, may hold values from 1.31528e-10 to 5.26112e-10
- gains_first: float32 [3, 256], replicated, may hold values from -0.00079786935 to 0.00079786935
- gains_second: float32 [3, 256], replicated, may hold values from 3.2882e-09 to 1.31528e-08
- owner_group: int32 [16, 2048, 1], P('dp'), may hold values from 0 to 15; in each aligned block of 2048 rows (0 to 2047, 2048 to 4095, ..., all dimensions but the last counted through in order) at most 256 rows name the same one
- row_offset: int32 [16, 2048], P('dp'), may hold values from 0 to 1567
- segment_ids: int32 [16, 1024], P('dp'), may hold values from 0 to 17, never falling along the last dimension, each value on 1 to 512 neighbouring positions
- live_slots: int32 [16], P('dp'), may hold values from 1 to 1024, as said below
- log_freq: float32 [16, 1024], P('dp'), may hold values from -2 to 0
Outputs:
- item_new: float32 [25088, 256], P(('dp', 'ffn'))
- item_first_new: float32 [25088, 256], P(('dp', 'ffn'))
- item_second_new: float32 [25088, 256], P(('dp', 'ffn'))
- attn_in_new: float32 [3, 256, 512], P(None, None, 'ffn')
- attn_in_first_new: float32 [3, 256, 512], P(None, None, 'ffn')
- attn_in_second_new: float32 [3, 256, 512], P(None, None, 'ffn')
- attn_out_new: float32 [512, 256], P('ffn')
- attn_out_first_new: float32 [512, 256], P('ffn')
- attn_out_second_new: float32 [512, 256], P('ffn')
- ffn_up_new: float32 [256, 1024], P(None, 'ffn')
- ffn_up_first_new: float32 [256, 1024], P(None, 'ffn')
- ffn_up_second_new: float32 [256, 1024], P(None, 'ffn')
- ffn_down_new: float32 [1024, 256], P('ffn')
- ffn_down_first_new: float32 [1024, 256], P('ffn')
- ffn_down_second_new: float32 [1024, 256], P('ffn')
- position_new: float32 [512, 256], replicated
- position_first_new: float32 [512, 256], replicated
- position_second_new: float32 [512, 256], replicated
- gains_new: float32 [3, 256], replicated
- gains_first_new: float32 [3, 256], replicated
- gains_second_new: float32 [3, 256], replicated
- loss_sum: float32 [], replicated
- live_count: float32 [], replicated
- grad_norm: float32 [], replicated
Inputs may be any that keep to these rules, and one draw needn't show every extreme that they name: `owner_group`: among the 2048 entries of one device, no group is named more than 256 times. `live_slots`: slots at or past a row's live count are padding. `segment_ids`: A segment is a run of at most 512 slots.
All inputs are finite; a program needn't handle non-finite values.
Results may differ from a plain program's by a relative error of at most 0.012.
The roundings to bfloat16 on the way count: a program that leaves them out, or rounds other values in their place, can miss the bound.
Values may be sent and summed in bfloat16 or wider, within the bound.
A program may use at most 192 MiB of HBM per device.

v0:
```python
import jax
import jax.numpy as jnp
from jax import lax
from jax.sharding import PartitionSpec as P

HEAD = 64
QBLOCK = 512
STEP = 10


EPSILON = 1e-05
SCALE = 0.125
CLIP = 1.0
RATE = 0.05
RATE_POSITION = 0.3
RATE_GAINS = 0.5
DECAY = 0.01
BETA_ONE = 0.9
BETA_TWO = 0.999
ADAM_EPS = 1e-08
LOWF = jnp.bfloat16
WIDE = jnp.float32


def norm_rows(value, gain):
    centred = value - jnp.mean(value, -1, keepdims=True)
    spread = jnp.mean(centred * centred, -1, keepdims=True)
    return centred * lax.rsqrt(spread + EPSILON) * gain


def norm_back(value, gain, grad):
    centred = value - jnp.mean(value, -1, keepdims=True)
    inverse = lax.rsqrt(jnp.mean(centred * centred, -1, keepdims=True) + EPSILON)
    unit = centred * inverse
    d_unit = grad * gain
    d_value = inverse * (
        d_unit
        - jnp.mean(d_unit, -1, keepdims=True)
        - unit * jnp.mean(d_unit * unit, -1, keepdims=True)
    )
    return (d_value, jnp.sum(grad * unit, 0))


def block_mask(segment, start, width):
    rows_q = start + jnp.arange(width, dtype=jnp.int32)
    cols = jnp.arange(segment.shape[0], dtype=jnp.int32)
    return (cols[None, :] <= rows_q[:, None]) & (
        segment[None, :] == segment[start : start + width][:, None]
    )


def split_heads(triple):
    heads = triple.shape[2] // HEAD
    return [triple[c].reshape(triple.shape[1], heads, HEAD) for c in range(3)]


def attend(triple, segment):
    query, keys, values = split_heads(triple)
    width = min(QBLOCK, query.shape[0])
    outputs, sums = ([], [])
    for start in range(0, query.shape[0], width):
        scores = (
            jnp.einsum(
                "qhe,khe->hqk", query[start : start + width], keys, preferred_element_type=WIDE
            )
            * SCALE
        )
        scores = jnp.where(block_mask(segment, start, width)[None], scores, -1e30)
        top = jnp.max(scores, -1, keepdims=True)
        expo = jnp.exp(scores - top)
        total = jnp.sum(expo, -1, keepdims=True)
        prob = (expo / total).astype(LOWF)
        outputs.append(
            jnp.einsum("hqk,khe->qhe", prob, values, preferred_element_type=WIDE).astype(LOWF)
        )
        sums.append(top + jnp.log(total))
    joined = jnp.concatenate(outputs, 0)
    return (joined.reshape(joined.shape[0], -1), jnp.concatenate(sums, 1))


def attend_back(triple, segment, sums, d_attended):
    query, keys, values = split_heads(triple)
    d_heads = d_attended.reshape(query.shape)
    width = min(QBLOCK, query.shape[0])
    d_query = []
    d_keys = jnp.zeros(keys.shape, WIDE)
    d_values = jnp.zeros(values.shape, WIDE)
    for start in range(0, query.shape[0], width):
        part = query[start : start + width]
        d_part = d_heads[start : start + width]
        scores = jnp.einsum("qhe,khe->hqk", part, keys, preferred_element_type=WIDE) * SCALE
        scores = jnp.where(block_mask(segment, start, width)[None], scores, -1e30)
        prob = jnp.exp(scores - sums[:, start : start + width])
        d_prob = jnp.einsum("qhe,khe->hqk", d_part, values, preferred_element_type=WIDE)
        d_scores = (prob * (d_prob - jnp.sum(prob * d_prob, -1, keepdims=True))).astype(LOWF)
        d_query.append(
            jnp.einsum("hqk,khe->qhe", d_scores, keys, preferred_element_type=WIDE) * SCALE
        )
        d_keys = (
            d_keys + jnp.einsum("hqk,qhe->khe", d_scores, part, preferred_element_type=WIDE) * SCALE
        )
        d_values = d_values + jnp.einsum(
            "hqk,qhe->khe", prob.astype(LOWF), d_part, preferred_element_type=WIDE
        )
    stacked = jnp.stack([jnp.concatenate(d_query, 0), d_keys, d_values])
    return stacked.reshape(3, query.shape[0], -1).astype(LOWF)


def layer_forward(rows, segment, live, logq, weights):
    attn_in, attn_out, ffn_up, ffn_down, position_table, norm_gains = weights
    slots = segment.shape[0]
    order = jnp.arange(slots, dtype=jnp.int32)
    before = jnp.concatenate([jnp.full((1,), -1, jnp.int32), segment[:-1]])
    place = order - lax.cummax(jnp.where(segment != before, order, 0), axis=0)
    alive = order < live
    first = rows[:slots].astype(WIDE) + jnp.take(position_table, place, axis=0)
    normed = norm_rows(first, norm_gains[0]).astype(LOWF)
    triple = jnp.einsum("td,cdf->ctf", normed, attn_in, preferred_element_type=WIDE).astype(LOWF)
    attended, sums = attend(triple, segment)
    second = first + lax.psum(jnp.dot(attended, attn_out, preferred_element_type=WIDE), "ffn")
    lifted = norm_rows(second, norm_gains[1]).astype(LOWF)
    inner = jnp.dot(lifted, ffn_up, preferred_element_type=WIDE)
    hidden = jax.nn.gelu(inner).astype(LOWF)
    third = second + lax.psum(jnp.dot(hidden, ffn_down, preferred_element_type=WIDE), "ffn")
    final = norm_rows(third, norm_gains[2]).astype(LOWF)
    logits = (
        jnp.einsum("id,jd->ij", final, rows[slots:], preferred_element_type=WIDE) - logq[None, :]
    )
    logits = jnp.where(alive[None, :], logits, -1e30)
    top = jnp.max(logits, -1, keepdims=True)
    expo = jnp.exp(logits - top)
    total = jnp.sum(expo, -1, keepdims=True)
    loss = jnp.sum(jnp.where(alive, top[:, 0] + jnp.log(total[:, 0]) - jnp.diagonal(logits), 0.0))
    identity = (order[:, None] == order[None, :]).astype(WIDE)
    grad_logits = ((expo / total - identity) * alive[:, None].astype(WIDE)).astype(LOWF)
    saved = (
        place,
        first,
        normed,
        triple,
        attended,
        sums,
        second,
        lifted,
        inner,
        hidden,
        third,
        final,
        grad_logits,
    )
    return (loss, saved)


def layer_backward(saved, candidates, segment, weights):
    attn_in, attn_out, ffn_up, ffn_down, position_table, norm_gains = weights
    (
        place,
        first,
        normed,
        triple,
        attended,
        sums,
        second,
        lifted,
        inner,
        hidden,
        third,
        final,
        grad_logits,
    ) = saved
    d_final = jnp.dot(grad_logits, candidates, preferred_element_type=WIDE)
    d_cand = jnp.einsum("ij,id->jd", grad_logits, final, preferred_element_type=WIDE)
    d_third, gain_three = norm_back(third, norm_gains[2], d_final)
    d_branch = d_third.astype(LOWF)
    grad_down = jnp.einsum("tf,td->fd", hidden, d_branch, preferred_element_type=WIDE)
    d_hidden = jnp.einsum("td,fd->tf", d_branch, ffn_down, preferred_element_type=WIDE)
    _, gelu_back = jax.vjp(jax.nn.gelu, inner)
    d_inner = gelu_back(d_hidden)[0].astype(LOWF)
    grad_up = jnp.einsum("td,tf->df", lifted, d_inner, preferred_element_type=WIDE)
    d_lifted = lax.psum(
        jnp.einsum("tf,df->td", d_inner, ffn_up, preferred_element_type=WIDE), "ffn"
    )
    d_lift_in, gain_two = norm_back(second, norm_gains[1], d_lifted)
    d_second = d_third + d_lift_in
    d_mixed = d_second.astype(LOWF)
    grad_out = jnp.einsum("tf,td->fd", attended, d_mixed, preferred_element_type=WIDE)
    d_attended = jnp.einsum("td,fd->tf", d_mixed, attn_out, preferred_element_type=WIDE).astype(
        LOWF
    )
    d_triple = attend_back(triple, segment, sums, d_attended)
    grad_in = jnp.einsum("td,ctf->cdf", normed, d_triple, preferred_element_type=WIDE)
    d_normed = lax.psum(
        jnp.einsum("ctf,cdf->td", d_triple, attn_in, preferred_element_type=WIDE), "ffn"
    )
    d_norm_in, gain_one = norm_back(first, norm_gains[0], d_normed)
    d_first = d_second + d_norm_in
    grad_position = jax.ops.segment_sum(d_first, place, position_table.shape[0])
    grads = (
        grad_in,
        grad_out,
        grad_up,
        grad_down,
        grad_position,
        jnp.stack([gain_one, gain_two, gain_three]),
    )
    return (jnp.concatenate([d_first, d_cand], 0), grads)


def fetch_rows(wanted, half_table, owners, ranks):
    held = half_table.shape[0]
    local = (
        lax.all_to_all(wanted, "dp", split_axis=0, concat_axis=0, tiled=True)
        - lax.axis_index("ffn") * held
    )
    valid = (local >= 0) & (local < held)
    picked = jnp.take(half_table, jnp.clip(local, 0, held - 1), axis=0)
    picked = jnp.where(valid[..., None], picked, jnp.zeros((), LOWF))
    arrived, local = (lax.all_to_all(picked, "dp", split_axis=0, concat_axis=0, tiled=True), local)
    whole = lax.psum(arrived, "ffn").astype(jnp.float32).astype(LOWF)
    return (whole[owners, ranks], local)


def adamw(weight, grad, first, second, decay, rate):
    first = BETA_ONE * first + (1.0 - BETA_ONE) * grad
    second = BETA_TWO * second + (1.0 - BETA_TWO) * grad * grad
    moved = first / (1.0 - BETA_ONE**STEP) / (jnp.sqrt(second / (1.0 - BETA_TWO**STEP)) + ADAM_EPS)
    return (weight - rate * (moved + decay * weight), first, second)


def body(
    item_table,
    attn_in,
    attn_out,
    ffn_up,
    ffn_down,
    position_table,
    norm_gains,
    item_first,
    item_second,
    attn_in_first,
    attn_in_second,
    attn_out_first,
    attn_out_second,
    ffn_up_first,
    ffn_up_second,
    ffn_down_first,
    ffn_down_second,
    position_first,
    position_second,
    gains_first,
    gains_second,
    owner_group,
    row_offset,
    segment_ids,
    live_slots,
    log_freq,
):
    groups = lax.axis_size("dp")
    halves = lax.axis_size("ffn")
    count_rows, slots = segment_ids.shape
    owners = owner_group.reshape(-1)
    offsets = row_offset.reshape(-1)
    capacity = 2 * owners.shape[0] // groups
    marks = (owners[:, None] == jnp.arange(groups, dtype=jnp.int32)[None, :]).astype(jnp.int32)
    ranks = jnp.sum(jnp.cumsum(marks, 0) * marks, 1) - 1
    wanted = jnp.full((groups, capacity), -1, jnp.int32).at[owners, ranks].set(offsets)
    half_table = item_table.astype(LOWF)
    weights = (
        attn_in.astype(LOWF),
        attn_out.astype(LOWF),
        ffn_up.astype(LOWF),
        ffn_down.astype(LOWF),
        position_table,
        norm_gains,
    )
    fetched, served = fetch_rows(wanted, half_table, owners, ranks)
    row = 0
    loss, saved = layer_forward(fetched, segment_ids[row], live_slots[row], log_freq[row], weights)
    kept = [saved]
    again, served_now = fetch_rows(wanted, half_table, owners, ranks)
    row = 0
    candidates = again[row * 2 * slots + slots : (row + 1) * 2 * slots]
    d_rows, grads = layer_backward(kept[row], candidates, segment_ids[row], weights)
    outgoing = (
        jnp.zeros((groups, capacity, item_table.shape[1]), WIDE).at[owners, ranks].set(d_rows)
    )
    incoming = lax.all_to_all(outgoing, "dp", split_axis=0, concat_axis=0, tiled=True)
    held = item_table.shape[0]
    valid = (served_now >= 0) & (served_now < held)
    grad_table = (
        jnp.zeros(item_table.shape, WIDE)
        .at[jnp.clip(served_now, 0, held - 1)]
        .add(jnp.where(valid[..., None], incoming, 0.0))
    )
    count_total = jnp.sum(live_slots).astype(WIDE)
    summed = lax.psum(
        (grads[0], grads[1], grads[2], grads[3], grads[4], grads[5], loss, count_total), "dp"
    )
    grad_in, grad_out, grad_up, grad_down, grad_position, grad_gains, loss_sum, live_count = summed
    split_sq = (
        jnp.sum(grad_in * grad_in)
        + jnp.sum(grad_out * grad_out)
        + jnp.sum(grad_up * grad_up)
        + jnp.sum(grad_down * grad_down)
    )
    shared_sq = jnp.sum(grad_position * grad_position) + jnp.sum(grad_gains * grad_gains)
    local_sq = jnp.sum(grad_table * grad_table) + split_sq / groups + shared_sq / (groups * halves)
    grad_norm = jnp.sqrt(lax.psum(local_sq, ("dp", "ffn")))
    factor = CLIP / jnp.maximum(grad_norm, CLIP)
    table_new = adamw(item_table, grad_table * factor, item_first, item_second, DECAY, RATE)
    in_new = adamw(attn_in, grad_in * factor, attn_in_first, attn_in_second, DECAY, RATE)
    out_new = adamw(attn_out, grad_out * factor, attn_out_first, attn_out_second, DECAY, RATE)
    up_new = adamw(ffn_up, grad_up * factor, ffn_up_first, ffn_up_second, DECAY, RATE)
    down_new = adamw(ffn_down, grad_down * factor, ffn_down_first, ffn_down_second, DECAY, RATE)
    position_new = adamw(
        position_table,
        grad_position * factor,
        position_first,
        position_second,
        DECAY,
        RATE_POSITION,
    )
    gains_new = adamw(norm_gains, grad_gains * factor, gains_first, gains_second, 0.0, RATE_GAINS)
    return (
        table_new[0],
        table_new[1],
        table_new[2],
        in_new[0],
        in_new[1],
        in_new[2],
        out_new[0],
        out_new[1],
        out_new[2],
        up_new[0],
        up_new[1],
        up_new[2],
        down_new[0],
        down_new[1],
        down_new[2],
        position_new[0],
        position_new[1],
        position_new[2],
        gains_new[0],
        gains_new[1],
        gains_new[2],
        loss_sum,
        live_count,
        grad_norm,
    )


def solution(mesh):
    return jax.shard_map(
        body,
        mesh=mesh,
        in_specs=(
            P(("dp", "ffn"), None),
            P(None, None, "ffn"),
            P("ffn", None),
            P(None, "ffn"),
            P("ffn", None),
            P(),
            P(),
            P(("dp", "ffn"), None),
            P(("dp", "ffn"), None),
            P(None, None, "ffn"),
            P(None, None, "ffn"),
            P("ffn", None),
            P("ffn", None),
            P(None, "ffn"),
            P(None, "ffn"),
            P("ffn", None),
            P("ffn", None),
            P(),
            P(),
            P(),
            P(),
            P("dp", None, None),
            P("dp", None),
            P("dp", None),
            P("dp"),
            P("dp", None),
        ),
        out_specs=(
            P(("dp", "ffn"), None),
            P(("dp", "ffn"), None),
            P(("dp", "ffn"), None),
            P(None, None, "ffn"),
            P(None, None, "ffn"),
            P(None, None, "ffn"),
            P("ffn", None),
            P("ffn", None),
            P("ffn", None),
            P(None, "ffn"),
            P(None, "ffn"),
            P(None, "ffn"),
            P("ffn", None),
            P("ffn", None),
            P("ffn", None),
            P(),
            P(),
            P(),
            P(),
            P(),
            P(),
            P(),
            P(),
            P(),
        ),
        check_vma=False,
    )
```

profile of v0, /device:TPU:0, one launch (start us, length us, event | category | flops | bytes accessed | tf_op | source)
XLA Modules:
  0.0 685.4 jit_solution(17691485908183172034)
XLA Ops:
  7.9 4.5 reduce-window.15
  16.2 8.8 %scatter_custom_fusion.2 = s32[4096]{0:T(1024)} fusion(s32[2048]{0:T(1024)S(1)} %broadcast_select_fusion.1, s32[2048]{0:T(1024)} %bitcast.199, s32[]{:T(128)} %constant.53.clone.1), kind=kCustom, calls=%fused_computation.181 | custom fusion | bytes 16896
  25.0 8.3 %all-to-all-start = ((s32[16,1,256]{2,1,0:T(1,128)}), s32[16,1,256]{2,1,0:T(1,128)S(1)}, u32[]{:S(2)}, u32[]{:S(2)}) async-start(s32[16,1,256]{2,1,0:T(1,128)} %bitcast.7), calls=%async_computation | async-start | bytes 32768 | tf_op jit(solution)/shard_map/all_to_all | solution.py:212
  34.6 6.1 all-to-all-done
  40.7 14.6 %gather_fusion.3 = bf16[4096,256]{1,0:T(8,128)(2,1)S(1)} fusion(bf16[784,256]{1,0:T(8,128)(2,1)S(1)} %convert_element_type.106, s32[4096]{0:T(1024)S(1)} %broadcast_clamp_fusion), kind=kCustom, calls=%fused_computation.clone | custom fusion | bytes 4210688 | tf_op jit(solution)/shard_map/jit(_take)/gather | solution.py:216
  56.8 51.2 %all_to_all.21 = bf16[16,256,256]{2,1,0:T(8,128)(2,1)} all-to-all(bf16[16,256,256]{2,1,0:T(8,128)(2,1)S(1)} %select_select_fusion), channel_id=1, replica_groups=mesh['dp'=16,'ffn'=2] {'dp'}, dimensions={0} | all-to-all | bytes 4194304 | tf_op jit(solution)/shard_map/all_to_all | solution.py:218
  114.4 13.3 %all-reduce.9.cloned.1.call-done = bf16[16,256,256]{2,1,0:T(8,128)(2,1)} async-done(((bf16[16,256,256]{2,1,0:T(8,128)(2,1)}), bf16[16,256,256]{2,1,0:T(8,128)(2,1)}) %all-reduce.9.cloned.1.call-update) | async-done | bytes 2097168 | tf_op jit(solution)/shard_map/psum | solution.py:219
  127.7 35.0 %gather_fusion = bf16[2048,256]{1,0:T(8,128)(2,1)} fusion(bf16[16,256,256]{2,1,0:T(8,128)(2,1)} %all-reduce.9.cloned.1.call-done, s32[2048]{0:T(1024)S(1)} %bitcast.142), kind=kCustom, calls=%fused_computation.1 | custom fusion | bytes 2113536 | tf_op jit(solution)/shard_map/gather | solution.py:220
  182.1 20.4 %all-reduce.11.cloned.1.call-done = f32[1024,256]{1,0:T(8,128)} async-done(((f32[1024,256]{1,0:T(8,128)}), f32[1024,256]{1,0:T(8,128)}) %all-reduce.11.cloned.1.call-update) | async-done | bytes 1048592 | tf_op jit(solution)/shard_map/psum | solution.py:120
  210.9 20.2 %all-reduce.13.cloned.1.call-done = f32[1024,256]{1,0:T(8,128)} async-done(((f32[1024,256]{1,0:T(8,128)}), f32[1024,256]{1,0:T(8,128)}) %all-reduce.13.cloned.1.call-update) | async-done | bytes 1048592 | tf_op jit(solution)/shard_map/psum | solution.py:124
  242.6 20.9 %all-reduce.15.cloned.1.call-done = f32[1024,256]{1,0:T(8,128)} async-done(((f32[1024,256]{1,0:T(8,128)}), f32[1024,256]{1,0:T(8,128)}) %all-reduce.15.cloned.1.call-update) | async-done | bytes 1048592 | tf_op jit(solution)/shard_map/psum | solution.py:180
  268.7 7.7 %multiply_reduce_fusion.1 = (f32[4,512]{1,0:T(4,128)S(1)}, f32[4,512,1024]{2,1,0:T(8,128)}) fusion(f32[4,512,1024]{2,1,0:T(8,128)} %copy-done.1, f32[4,512]{1,0:T(4,128)S(1)} %log_add_fusion.1, bf16[512,4,64]{0,2,1:T(8,128)(2,1)S(1)} %bitcast.162, bf16[1024,4,64]{0,2,1:T(8,128)(2,1)S(1)} %bitcast.154), kind=kOutput, calls=%fused_computation.12 | convolution fusion | flops 274724864 | bytes 17580032 | tf_op jit(solution)/shard_map/qhe,khe->hqk/dot_general | solution.py:94
  276.4 4.5 multiply_convert_fusion.1
  286.6 4.3 multiply_reduce_fusion
  295.3 6.7 multiply_convert_fusion
  315.3 17.2 %all-reduce.17.cloned.1.call-done = f32[1024,256]{1,0:T(8,128)} async-done(((f32[1024,256]{1,0:T(8,128)}), f32[1024,256]{1,0:T(8,128)}) %all-reduce.17.cloned.1.call-update) | async-done | bytes 1048592 | tf_op jit(solution)/shard_map/psum | solution.py:192
  337.4 12.0 %scatter_custom_fusion.3 = f32[4096,256]{1,0:T(8,128)} fusion(s32[2048]{0:T(1024)S(1)} %broadcast_select_fusion.1, f32[1024,256]{1,0:T(8,128)} %fusion.90, f32[]{:T(128)} %constant.70.clone.1, f32[1024,256]{1,0:T(8,128)} %multiply_add_fusion, f32[]{:T(128)} %constant.51.clone.1), kind=kCustom, calls=%fused_computation.44 | custom fusion | flops 524288 | bytes 6291464
  349.5 6.8 all-to-all-start.2
  366.0 7.4 %scatter_custom_fusion.1 = f32[512,256]{1,0:T(8,128)} fusion(s32[1024]{0:T(1024)S(1)} %bitcast.197, f32[1024,256]{1,0:T(8,128)} %multiply_add_fusion, f32[]{:T(128)} %constant.51.clone.1), kind=kCustom, calls=%fused_computation.136 | custom fusion | flops 262144 | bytes 524800 | tf_op jit(solution)/shard_map/scatter-add | solution.py:197
  374.0 17.2 %gather_fusion.2 = f32[1024]{0:T(1024)S(1)} fusion(f32[1024,1024]{0,1:T(8,128)} %copy-done.3, s32[1024]{0:T(1024)S(1)} %bitcast.143), kind=kCustom, calls=%fused_computation.3 | custom fusion | bytes 16384 | tf_op jit(solution)/shard_map/jit(diagonal)/cond/branch_0_fun/gather | solution.py:133
  391.8 92.8 %all-reduce = (f32[3,256]{1,0:T(4,128)S(1)}, f32[]{:T(128)}, f32[]{:T(128)}) all-reduce(f32[3,256]{1,0:T(4,128)S(1)} %pad_maximum_fusion.5, f32[]{:T(128)} %select_reduce_fusion, f32[]{:T(128)S(6)} %convert_element_type.135), channel_id=1, replica_groups=mesh['dp'=16,'ffn'=2] {'dp'}, use_global_device_ids=true, to_apply=%region_48.50 | all-reduce | flops 770 | bytes 6160 | tf_op jit(solution)/shard_map/psum | solution.py:296
  485.2 82.5 %all-reduce.19.cloned.1.call-done = (f32[3,256,256]{1,2,0:T(8,128)}, f32[256,256]{1,0:T(8,128)}, f32[256,512]{1,0:T(8,128)}, f32[512,256]{1,0:T(8,128)}, f32[512,256]{1,0:T(8,128)}) async-done(((f32[3,256,256]{1,2,0:T(8,128)}, f32[256,256]{1,0:T(8,128)}, f32[256,512]{1,0:T(8,128)}, f32[512,256]{1,0:T(8,128)}, f32[512,256]{1,0:T(8,128)}), (f32[3,256,256]{1,2,0:T(8,128)}, f32[256,256]{1,0:T(8,128)}, ...) | async-done | bytes 2621456 | tf_op jit(solution)/shard_map/psum | solution.py:296
  584.6 26.8 %scatter_custom_fusion = f32[784,256]{1,0:T(8,128)S(1)} fusion(s32[4096]{0:T(1024)S(1)} %bitcast.188, f32[4096,256]{1,0:T(8,128)} %bitcast.156, f32[]{:T(128)} %constant.51.clone.1), kind=kCustom, calls=%fused_computation.130 | custom fusion | flops 1048576 | bytes 803328 | tf_op jit(solution)/shard_map/scatter-add | solution.py:293
  615.2 39.2 %psum.112 = f32[]{:T(128)} all-reduce(f32[]{:T(128)S(6)} %add.356), channel_id=1, replica_groups=mesh['dp'=16,'ffn'=2] {'dp','ffn'}, use_global_device_ids=true, to_apply=%region_50.52 | all-reduce | flops 1 | bytes 8 | tf_op jit(solution)/shard_map/psum | solution.py:308
  (238 shorter events, 134.5 us)
Async XLA Ops:
  25.0 15.7 %all-to-all-start = ((s32[16,1,256]{2,1,0:T(1,128)}), s32[16,1,256]{2,1,0:T(1,128)S(1)}, u32[]{:S(2)}, u32[]{:S(2)}) async-start(s32[16,1,256]{2,1,0:T(1,128)} %bitcast.7), calls=%async_computation | async-start | bytes 32768 | tf_op jit(solution)/shard_map/all_to_all | solution.py:212
  33.3 94.4 %all-reduce.9.cloned.1.call-start = ((), (), s32[]{:S(2)}) async-start(), calls=%async_computation.3 | async-start | bytes 4194304 | tf_op jit(solution)/shard_map/psum | solution.py:219
  56.8 51.6 %copy-start.43 = (s32[1,1024]{1,0:T(1,128)S(1)}, s32[1,1024]{1,0:T(1,128)}, u32[]{:S(2)}) copy-start(s32[1,1024]{1,0:T(1,128)} %param.51) | copy-start | bytes 12292
  56.8 52.3 %copy-start.2 = (f32[512,256]{1,0:T(8,128)S(1)}, f32[512,256]{1,0:T(8,128)}, u32[]{:S(2)}) copy-start(f32[512,256]{1,0:T(8,128)} %param.33) | copy-start | bytes 1572868
  108.0 94.5 %all-reduce.11.cloned.1.call-start = ((), (), s32[]{:S(2)}) async-start(), calls=%async_computation.4 | async-start | bytes 2097152 | tf_op jit(solution)/shard_map/psum | solution.py:120
  165.7 10.9 %copy-start.10 = (bf16[1,1024,256]{1,2,0:T(8,128)(2,1)}, bf16[1,1024,256]{1,2,0:T(8,128)(2,1)S(1)}, u32[]{:S(2)}) copy-start(bf16[1,1024,256]{1,2,0:T(8,128)(2,1)S(1)} %get-tuple-element.172) | copy-start | bytes 1572868
  181.5 49.6 %all-reduce.13.cloned.1.call-start = ((), (), s32[]{:S(2)}) async-start(), calls=%async_computation.5 | async-start | bytes 2097152 | tf_op jit(solution)/shard_map/psum | solution.py:124
  207.2 25.8 %copy-start.47 = (f32[1,1024]{1,0:T(1,128)S(1)}, f32[1,1024]{1,0:T(1,128)}, u32[]{:S(2)}) copy-start(f32[1,1024]{1,0:T(1,128)} %param.53) | copy-start | bytes 12292
  210.2 53.3 %all-reduce.15.cloned.1.call-start = ((), (), s32[]{:S(2)}) async-start(), calls=%async_computation.6 | async-start | bytes 2097152 | tf_op jit(solution)/shard_map/psum | solution.py:180
  242.5 90.0 %all-reduce.17.cloned.1.call-start = ((), (), s32[]{:S(2)}) async-start(), calls=%async_computation.7 | async-start | bytes 2097152 | tf_op jit(solution)/shard_map/psum | solution.py:192
  276.4 8.5 %slice-start = ((s8[8388608]{0:T(1024)(128)(4,1)}), s8[4194304]{0:T(1024)(128)(4,1)S(1)}, s32[]{:S(2)}) async-start(s8[8388608]{0:T(1024)(128)(4,1)} %bitcast.138), calls=%async_computation.9 | async-start | bytes 8388608
  276.4 8.5 %slice-start.1 = ((s8[8388608]{0:T(1024)(128)(4,1)}), s8[4194304]{0:T(1024)(128)(4,1)S(1)}, s32[]{:S(2)}) async-start(s8[8388608]{0:T(1024)(128)(4,1)} %bitcast.138), calls=%async_computation.10 | async-start | bytes 8388608
  349.5 231.0 %all-to-all-start.2 = ((f32[16,256,256]{2,1,0:T(8,128)}), f32[16,256,256]{2,1,0:T(8,128)}, u32[]{:S(2)}, u32[]{:S(2)}) async-start(f32[16,256,256]{2,1,0:T(8,128)} %bitcast.144), calls=%async_computation.2 | async-start | bytes 8388608 | tf_op jit(solution)/shard_map/all_to_all | solution.py:287
  356.3 211.3 %all-reduce.19.cloned.1.call-start = ((), (), s32[]{:S(2)}) async-start(), calls=%async_computation.8 | async-start | bytes 5242880 | tf_op jit(solution)/shard_map/psum | solution.py:296
  364.1 9.2 %copy-start.20 = (f32[3,256,256]{2,1,0:T(8,128)S(1)}, f32[3,256,256]{2,1,0:T(8,128)}, u32[]{:S(2)}) copy-start(f32[3,256,256]{2,1,0:T(8,128)} %param.29) | copy-start | bytes 2359300
  655.2 10.2 %copy-start.45 = (f32[3,256]{1,0:T(4,128)S(1)}, f32[3,256]{1,0:T(4,128)}, u32[]{:S(2)}) copy-start(f32[3,256]{1,0:T(4,128)} %param.47) | copy-start | bytes 9220
  655.2 10.2 %copy-start.46 = (f32[3,256]{1,0:T(4,128)S(1)}, f32[3,256]{1,0:T(4,128)}, u32[]{:S(2)}) copy-start(f32[3,256]{1,0:T(4,128)} %param.48) | copy-start | bytes 9220
  655.2 10.8 %copy-start.24 = (f32[256,256]{1,0:T(8,128)S(1)}, f32[256,256]{1,0:T(8,128)}, u32[]{:S(2)}) copy-start(f32[256,256]{1,0:T(8,128)} %param.30) | copy-start | bytes 786436
  658.4 9.9 %copy-start.32 = (f32[512,256]{1,0:T(8,128)S(1)}, f32[512,256]{1,0:T(8,128)}, u32[]{:S(2)}) copy-start(f32[512,256]{1,0:T(8,128)} %get-tuple-element.137) | copy-start | bytes 1572868
  660.7 10.1 %copy-start.31 = (f32[512,256]{1,0:T(8,128)S(1)}, f32[512,256]{1,0:T(8,128)}, u32[]{:S(2)}) copy-start(f32[512,256]{1,0:T(8,128)} %get-tuple-element.136) | copy-start | bytes 1572868
  666.0 7.8 %copy-start.13 = (f32[256,512]{1,0:T(8,128)S(1)}, f32[256,512]{1,0:T(8,128)}, u32[]{:S(2)}) copy-start(f32[256,512]{1,0:T(8,128)} %param.31) | copy-start | bytes 1572868
  666.0 7.8 %copy-start.30 = (f32[256,512]{1,0:T(8,128)S(1)}, f32[256,512]{1,0:T(8,128)}, u32[]{:S(2)}) copy-start(f32[256,512]{1,0:T(8,128)} %get-tuple-element.135) | copy-start | bytes 1572868
  666.0 7.8 %copy-start.41 = (f32[256,512]{1,0:T(8,128)S(1)}, f32[256,512]{1,0:T(8,128)}, u32[]{:S(2)}) copy-start(f32[256,512]{1,0:T(8,128)} %param.41) | copy-start | bytes 1572868
  666.0 7.8 %copy-start.42 = (f32[256,512]{1,0:T(8,128)S(1)}, f32[256,512]{1,0:T(8,128)}, u32[]{:S(2)}) copy-start(f32[256,512]{1,0:T(8,128)} %param.42) | copy-start | bytes 1572868
  (36 other events, 127.0 us)
Sparse Core Ops, SparseCore 0:
  108.1 19.5 all-reduce.8
  181.7 20.7 all-reduce.10
  210.3 20.7 all-reduce.12
  242.6 20.7 all-reduce.14
  311.7 20.7 all-reduce.16
  373.5 194.1 all-reduce.18
where the time goes:
time: 691 us; the launch traced here: 685 us
  blocking collectives  183 us (26%)
  waiting for transfers between devices  181 us (26%)
  other arithmetic  123 us (18%)
  local copies, waits for them, and re-layouts  101 us (15%)
  matrix products  59.1 us (9%)
  between operations  22.4 us (3%)
  starting transfers between devices  16.2 us (2%)
    psum x1, blocking collectives, body(): lax.psum((grads[0], grads[1], grads[2], grads[3], grads[4], grads[5], los...  92.8 us
    psum x1, waiting for transfers between devices, body(): lax.psum((grads[0], grads[1], grads[2], grads[3], grads[4], grads[5], los...  82.5 us
    all_to_all x1, blocking collectives, fetch_rows(): lax.all_to_all(picked, 'dp', split_axis=0, concat_axis=0, tiled=True)  51.2 us
    psum x1, blocking collectives, body(): grad_norm = jnp.sqrt(lax.psum(local_sq, ('dp', 'ffn')))  39.2 us
    gather x1, local copies, waits for them, and re-layouts, fetch_rows(): return (whole[owners, ranks], local)  35 us
    scatter-add x1, other arithmetic, body(): grad_table = jnp.zeros(item_table.shape, WIDE).at[jnp.clip(served_now, 0,...  26.8 us
    unnamed x113, local copies, waits for them, and re-layouts  25.1 us
    psum x1, waiting for transfers between devices, layer_backward(): lax.psum(jnp.einsum('tf,df->td', d_inner, ffn_up, preferred_element_type=...  20.9 us
  transfers between devices with their start and end apart: 8, of which 7 were waited for; matrix products, arithmetic and copies ran while one was open for 8% of the time, Pallas kernels for 0%

commit v1 on v0

v1 whole, which is shorter than its diff:
```python
import functools
import types

import jax
import jax.numpy as jnp
from jax import lax
from jax.experimental import pallas as pl
from jax.experimental.pallas import tpu as pltpu
from jax.sharding import PartitionSpec as P

HEAD = 64
STEP = 10
EPSILON = 1e-05
SCALE = 0.125
CLIP = 1.0
RATE = 0.05
RATE_POSITION = 0.3
RATE_GAINS = 0.5
DECAY = 0.01
BETA_ONE = 0.9
BETA_TWO = 0.999
ADAM_EPS = 1e-08
GELU_A = 0.7978845608028654
GELU_B = 0.044715
LOWF = jnp.bfloat16
WIDE = jnp.float32
MESH = pl.DeviceIdType.MESH
DMA = pltpu.SemaphoreType.DMA
VMEM = pl.BlockSpec(memory_space=pltpu.VMEM)
SMEM = pl.BlockSpec(memory_space=pltpu.SMEM)
FAR = pl.BlockSpec(memory_space=pltpu.HBM)
TILE = 128
GROUP = 256
NN = (((1,), (0,)), ((), ()))
NT = (((1,), (1,)), ((), ()))
TN = (((0,), (0,)), ((), ()))
LOWEST = -1e30
REACH = 4
LEVELS = 32
LINKS = 24


def tile_iota(shape, axis):
    return lax.broadcasted_iota(jnp.int32, shape, axis)


def matmul(left, right, dims=NN):
    return lax.dot_general(left, right, dims, preferred_element_type=WIDE)


def as_column(row, eye, ones):
    return matmul((eye * row).astype(LOWF), ones)


def one_hot(condition):
    return jnp.where(condition, 1.0, 0.0).astype(LOWF)


def span(start, size, unit=16):
    return pl.ds(pl.multiple_of(start, unit), size)


def over(count, step):
    def run(index, carry):
        step(index)
        return carry

    lax.fori_loop(0, count, run, 0)


def flipped(value, mask, bits=4):
    total = 0
    for bit in range(bits):
        one, two = (value // 2**bit) % 2, (mask // 2**bit) % 2
        total = total + (one + two - 2 * one * two) * 2**bit
    return total


def copy_to(source, target, send_sem, recv_sem, where):
    return pltpu.make_async_remote_copy(
        src_ref=source,
        dst_ref=target,
        send_sem=send_sem,
        recv_sem=recv_sem,
        device_id=where,
        device_id_type=MESH,
    )


def send(source, target, send_sem, recv_sem, where):
    copy_to(source, target, send_sem, recv_sem, where).start()


def spread_rows(value):
    centred = value - jnp.mean(value, -1, keepdims=True)
    inverse = lax.rsqrt(jnp.mean(centred * centred, -1, keepdims=True) + EPSILON)
    return centred * inverse, inverse


def spread_back(unit, inverse, gain, grad):
    d_unit = grad * gain
    return inverse * (
        d_unit
        - jnp.mean(d_unit, -1, keepdims=True)
        - unit * jnp.mean(d_unit * unit, -1, keepdims=True)
    )


def windows(slots):
    found, at = [], 0
    for block in range(slots // TILE):
        low = max(0, block - REACH) * TILE
        width = (block + 1) * TILE - low
        found.append((block, low, width, at))
        at += width
    return found, at


def levels_of(groups):
    inner = 4 if groups % 4 == 0 else 1
    return inner, groups // inner


def shard_rows(rows, groups):
    return -(-rows // (groups * 16)) * 16


def part_scratch(name, rows, width, groups):
    inner, outer = levels_of(groups)
    shard = shard_rows(rows, groups)
    return {
        name + "_source": pltpu.VMEM((groups * shard, width), LOWF),
        name + "_plane": pltpu.VMEM((inner, outer * shard, width), LOWF),
        name + "_half": pltpu.VMEM((outer * shard, width), LOWF),
        name + "_column": pltpu.VMEM((outer, shard, width), LOWF),
        name + "_shard": pltpu.VMEM((shard, width), WIDE),
        name + "_plane_sent": DMA((inner,)),
        name + "_plane_came": DMA((inner,)),
        name + "_column_sent": DMA((outer,)),
        name + "_column_came": DMA((outer,)),
        name + "_out_sent": DMA((outer,)),
        name + "_ahead_sent": DMA((groups,)),
        name + "_came": DMA((groups,)),
    }


class Part:
    def __init__(self, scratch, name, whole, groups, me, core):
        for key, ref in vars(scratch).items():
            if key.startswith(name + "_"):
                setattr(self, key[len(name) + 1 :], ref)
        self.whole, self.me, self.core = whole, me, core
        self.inner, self.outer = levels_of(groups)
        self.i, self.o = me % self.inner, me // self.inner
        self.size = self.shard.shape[0]

    def quarter(self, j):
        return span(j * self.outer * self.size, self.outer * self.size)

    def piece(self, j, o):
        return span((j * self.outer + o) * self.size, self.size)

    def plane_copy(self, j):
        return copy_to(
            self.source.at[self.quarter(j)],
            self.plane.at[self.i],
            self.plane_sent.at[j],
            self.plane_came.at[self.i],
            (self.o * self.inner + j, self.core),
        )

    def column_copy(self, o):
        return copy_to(
            self.half.at[span(o * self.size, self.size)],
            self.column.at[self.o],
            self.column_sent.at[o],
            self.column_came.at[self.o],
            (o * self.inner + self.i, self.core),
        )

    def out_copy(self, o):
        block = self.whole.at[self.piece(self.i, self.o)]
        came = self.came.at[self.i * self.outer + self.o]
        return copy_to(block, block, self.out_sent.at[o], came, (o * self.inner + self.i, self.core))

    def ahead_copy(self, o, j):
        block = self.whole.at[self.piece(self.i, o)]
        came = self.came.at[self.i * self.outer + o]
        sent = self.ahead_sent.at[j * self.outer + o]
        return copy_to(block, block, sent, came, (self.o * self.inner + j, self.core))

    def wait(self, ref, semaphore):
        copy_to(ref, ref, semaphore, semaphore, (self.me, self.core)).wait_recv()

    def start(self):
        over(self.inner - 1, lambda k: self.plane_copy((self.i + k + 1) % self.inner).start())

    def across(self):
        total = self.source[self.quarter(self.i), :].astype(WIDE)
        for k in range(self.inner - 1):
            j = (self.i + k + 1) % self.inner
            self.wait(self.plane.at[j], self.plane_came.at[j])
            total = total + self.plane[j].astype(WIDE)
        self.half[...] = total.astype(LOWF)
        over(self.outer - 1, lambda k: self.column_copy((self.o + k + 1) % self.outer).start())

    def settle(self):
        self.shard[...] = self.half[span(self.o * self.size, self.size), :].astype(WIDE)

        def take(k):
            o = (self.o + k + 1) % self.outer
            self.wait(self.column.at[o], self.column_came.at[o])
            self.shard[...] += self.column[o].astype(WIDE)

        over(self.outer - 1, take)
        self.whole[self.piece(self.i, self.o), :] = self.shard[...].astype(LOWF)
        over(self.outer - 1, lambda k: self.out_copy((self.o + k + 1) % self.outer).start())
        self.pass_on(self.o)

    def pass_on(self, o):
        over(self.inner - 1, lambda k: self.ahead_copy(o, (self.i + k + 1) % self.inner).start())

    def forward(self):
        def step(k):
            o = (self.o + k + 1) % self.outer
            block = self.whole.at[self.piece(self.i, o)]
            self.wait(block, self.came.at[self.i * self.outer + o])
            self.pass_on(o)

        over(self.outer - 1, step)

    def collect(self):
        def step(k):
            j = (self.i + k // self.outer + 1) % self.inner
            o = k % self.outer
            block = self.whole.at[self.piece(j, o)]
            self.wait(block, self.came.at[j * self.outer + o])

        over((self.inner - 1) * self.outer, step)

    def drain(self):
        over(self.inner - 1, lambda k: self.plane_copy((self.i + k + 1) % self.inner).wait_send())

        def far(k):
            o = (self.o + k + 1) % self.outer
            self.column_copy(o).wait_send()
            self.out_copy(o).wait_send()

        over(self.outer - 1, far)

        def near(k):
            j = (self.i + k // self.outer + 1) % self.inner
            self.ahead_copy(k % self.outer, j).wait_send()

        over((self.inner - 1) * self.outer, near)


def step_scratch(groups, held, entries, width, heads_width, hidden, places):
    slots = entries // 2
    own = slots // 2
    pairs = heads_width // TILE
    area = windows(slots)[1]
    blocks = slots // TILE
    padded = -(-2 * held // TILE) * TILE
    shapes = {
        "table": ((padded, width), LOWF),
        "flat": ((1, entries), jnp.int32),
        "column": ((slots, TILE), WIDE),
        "want": ((groups, 8, TILE), jnp.int32),
        "asked": ((groups, 8, TILE), jnp.int32),
        "reqs": ((2, entries // TILE, TILE), jnp.int32),
        "leaving": ((entries, width), LOWF),
        "arrived": ((2, entries, width), LOWF),
        "cands": ((slots, width), LOWF),
        "w_out": ((2, heads_width, width), LOWF),
        "w_up": ((2, width, hidden), LOWF),
        "w_down": ((2, hidden, width), LOWF),
        "w_in": ((3, width, heads_width), LOWF),
        "segments": ((slots, TILE), WIDE),
        "place": ((slots, TILE), WIDE),
        "place_row": ((1, slots), jnp.int32),
        "bias": ((area, TILE), WIDE),
        "pos_high": ((places, width), LOWF),
        "pos_low": ((places, width), LOWF),
        "first": ((own, width), WIDE),
        "normed": ((slots, width), LOWF),
        "normed_t": ((width, slots), LOWF),
        "queries": ((pairs, blocks, 2 * TILE, TILE), LOWF),
        "keys": ((pairs, slots, TILE), LOWF),
        "values": ((pairs, slots, TILE), LOWF),
        "keys_t": ((pairs, TILE, slots), LOWF),
        "values_t": ((pairs, TILE, slots), LOWF),
        "probs": ((pairs, area, 2 * TILE), WIDE),
        "mixed": ((pairs, slots, TILE), LOWF),
        "mixed_in": ((pairs, own, TILE), LOWF),
        "joined": ((2, own, heads_width), LOWF),
        "unit_zero": ((own, width), WIDE),
        "inverse_zero": ((own, TILE), WIDE),
        "unit_one": ((own, width), WIDE),
        "inverse_one": ((own, TILE), WIDE),
        "lifted": ((own, width), LOWF),
        "hidden": ((2, own, hidden), LOWF),
        "unit_two": ((own, width), WIDE),
        "inverse_two": ((own, TILE), WIDE),
        "final": ((own, width), LOWF),
        "logit_bias": ((1, slots), WIDE),
        "d_logits": ((own, slots), LOWF),
        "d_third": ((own, width), WIDE),
        "d_branch": ((own, width), LOWF),
        "d_inner": ((2, own, hidden), LOWF),
        "d_second": ((own, width), WIDE),
        "d_mixed": ((own, width), LOWF),
        "d_heads": ((pairs, slots, TILE), LOWF),
        "d_heads_out": ((pairs, own, TILE), LOWF),
        "d_cand": ((slots * width // TILE, TILE), WIDE),
        "g_out": ((2, heads_width, width), WIDE),
        "g_up": ((2, width, hidden), WIDE),
        "g_down": ((2, hidden, width), WIDE),
        "g_out_in": ((heads_width, width), WIDE),
        "g_up_in": ((width, hidden), WIDE),
        "g_down_in": ((hidden, width), WIDE),
        "d_keys": ((pairs, slots, TILE), WIDE),
        "d_values": ((pairs, slots, TILE), WIDE),
        "d_triple": ((3, slots, heads_width), LOWF),
        "d_normed_in": ((own, width), WIDE),
        "d_rows": ((entries, width), LOWF),
        "few": ((8, width), WIDE),
        "few_in": ((8, width), WIDE),
        "few_all": ((groups, 8, width), WIDE),
        "landed": ((2, entries, width), LOWF),
        "squares": ((2 * groups, 8, TILE), WIDE),
        "early_whole": ((groups * shard_rows(2 * hidden + heads_width, groups), width), LOWF),
        "late_whole": ((groups * shard_rows(3 * heads_width + places // 2, groups), width), LOWF),
        "other_half": ((places // 2, width), LOWF),
    }
    scratch = {name: pltpu.VMEM(*entry) for name, entry in shapes.items()}
    for name in ("want", "row", "few", "land"):
        scratch[name + "_sent"] = DMA((groups,))
        scratch[name + "_came"] = DMA((groups,))
    for name in ("pass", "hand"):
        scratch[name + "_sent"] = DMA((entries // GROUP,))
        scratch[name + "_came"] = DMA((entries // GROUP,))
    scratch["square_sent"] = DMA((2 * groups,))
    scratch["square_came"] = DMA((2 * groups,))
    scratch["sent"] = DMA((LINKS,))
    scratch["came"] = DMA((LINKS,))
    scratch["loads"] = DMA((12,))
    scratch.update(part_scratch("early", 2 * hidden + heads_width, width, groups))
    scratch.update(part_scratch("late", 3 * heads_width + places // 2, width, groups))
    return scratch


def step_kernel(groups, names, *refs):
    (table_far, in_far, out_far, up_far, down_far, pos_far) = refs[:6]
    (own_ref, off_ref, seg_ref, live_ref, logq_ref, gain_ref) = refs[6:12]
    (table_ref, early_ref, late_ref, position_ref, few_ref, stats_ref) = refs[12:18]
    s = types.SimpleNamespace(**dict(zip(names, refs[18:])))
    me, core = lax.axis_index("dp"), lax.axis_index("ffn")
    other = 1 - core
    held, width = table_far.shape
    entries = own_ref.shape[1]
    slots = entries // 2
    own = slots // 2
    half = entries // groups
    share = TILE // half
    tiles = entries // TILE
    spans = entries // GROUP
    pairs, hidden, places = s.keys.shape[0], s.w_up.shape[2], pos_far.shape[0]
    heads_width = pairs * TILE
    mine, yours = span(core * own, own), span(other * own, own)
    early = Part(s, "early", s.early_whole, groups, me, core)
    late = Part(s, "late", s.late_whole, groups, me, core)

    barrier = pltpu.get_barrier_semaphore()
    slot_of = me * 2 + core

    def greet(k):
        where = (slot_of + k + 1) % (2 * groups)
        pl.semaphore_signal(
            barrier, inc=1, device_id=(where // 2, where % 2), device_id_type=MESH
        )

    over(2 * groups - 1, greet)
    spare = s.probs.at[0]
    s.d_cand_in = s.bias.at[pl.ds(0, slots * width // TILE)]
    s.total = s.d_normed = s.probs.at[1, pl.ds(0, slots)]
    s.grad_table = spare.at[pl.ds(0, held)]
    pieces = [table_far, out_far]
    pieces += [up_far.at[:, pl.ds(c * width, width)] for c in range(hidden // width)]
    pieces += [down_far, *(in_far.at[c] for c in range(3)), pos_far]
    loads, staged, at = [], [], 0
    for index, piece in enumerate(pieces):
        near = spare.at[pl.ds(at, piece.shape[0])]
        at += piece.shape[0]
        staged.append(near)
        loads.append(pltpu.make_async_copy(piece, near, s.loads.at[index]))
    for load in loads:
        load.start()

    def swap(index, source, target):
        send(source, target, s.sent.at[index], s.came.at[index], (me, other))

    def arrived(ref, semaphore):
        copy_to(ref, ref, semaphore, semaphore, (me, core)).wait_recv()

    def departed(ref, semaphore):
        copy_to(ref, ref, semaphore, semaphore, (me, core)).wait_send()

    def swapped(index, target):
        arrived(target, s.came.at[index])

    upper = one_hot(tile_iota((GROUP, GROUP), 0) <= tile_iota((GROUP, GROUP), 1))
    group_of = tile_iota((groups, GROUP), 0)
    before = jnp.zeros((groups, 1), WIDE)
    filled = jnp.zeros((3 * groups, TILE), WIDE)
    spot = (me % share) * half - core * half
    for chunk in range(spans):
        at = slice(chunk * GROUP, (chunk + 1) * GROUP)
        owner, offset = own_ref[:, at], off_ref[:, at]
        marks = jnp.where(group_of == owner, 1.0, 0.0)
        running = matmul(marks.astype(LOWF), upper) + before
        before = running[:, GROUP - 1 :]
        ranks = (jnp.sum(marks * running, 0, keepdims=True) - 1.0).astype(jnp.int32)
        slot = owner * half + ranks
        s.flat[:, at] = jnp.where(ranks < half, slot, slot + (entries - half))
        inside = (ranks >= core * half) & (ranks < core * half + half)
        picks = one_hot(tile_iota((TILE, GROUP), 0) == jnp.where(inside, ranks + spot, -1))
        parts = jnp.concatenate(
            [
                marks * lax.shift_right_logical(offset, 6).astype(WIDE),
                marks * (offset & 63).astype(WIDE),
                marks,
            ],
            0,
        ).astype(LOWF)
        filled = filled + matmul(parts, picks, NT)
    asking = (
        64.0 * filled[:groups] + filled[groups : 2 * groups] + filled[2 * groups :]
    ).astype(jnp.int32)
    for owner in range(groups):
        s.want[owner] = jnp.broadcast_to(asking[owner : owner + 1], (8, TILE))
    s.asked[me] = s.want[me]
    pl.semaphore_wait(barrier, 2 * groups - 1)

    def ask(k):
        owner = (me + groups // 2 + k) % groups

        @pl.when(owner != me)
        def _():
            send(
                s.want.at[owner], s.asked.at[me], s.want_sent.at[owner], s.want_came.at[me], (owner, core)
            )

    over(groups, ask)
    rows_mine, rows_yours = span(core * held, held), span(other * held, held)
    loads[0].wait()
    s.table[rows_mine, :] = staged[0][...].astype(LOWF)
    s.table[2 * held :, :] = jnp.zeros((s.table.shape[0] - 2 * held, width), LOWF)
    swap(0, s.table.at[rows_mine], s.table.at[rows_mine])
    eye = (tile_iota((TILE, TILE), 0) == tile_iota((TILE, TILE), 1)).astype(WIDE)
    ones = jnp.ones((TILE, TILE), LOWF)

    def column_of(line):
        return 64.0 * as_column(lax.shift_right_logical(line, 6).astype(WIDE), eye, ones) + as_column(
            (line & 63).astype(WIDE), eye, ones
        )

    for chunk in range(slots // TILE):
        side, at = divmod(chunk * TILE, own)
        line = s.flat[:, span(side * slots + core * own + at, TILE, TILE)]
        s.column[chunk * TILE : (chunk + 1) * TILE, :] = column_of(line)
    s.total[...] = jnp.zeros(s.total.shape, WIDE)
    swapped(0, s.table.at[rows_yours])
    lanes_wide = tile_iota((TILE, TILE), 1).astype(WIDE)

    def serve(k):
        tile = flipped(me // share, tiles - 1 - k)
        line = jnp.zeros((1, TILE), jnp.int32)
        for j in range(share):
            source = tile * share + j

            @pl.when(source != me)
            def _():
                arrived(s.asked.at[source], s.want_came.at[source])

        for j in range(share):
            line = line + s.asked[tile * share + j][0:1, :]
        s.reqs[core, pl.ds(tile, 1), :] = line
        number = column_of(line)
        hot = jnp.concatenate(
            [
                one_hot(number == lanes_wide + float(b * TILE + 1))
                for b in range(s.table.shape[0] // TILE)
            ],
            1,
        )
        picked = matmul(hot, s.table[...]).astype(LOWF)
        s.leaving[span(tile * TILE, TILE), :] = picked
        into = s.arrived.at[core, span(me * half, half)]
        for j in range(share):
            source = tile * share + j
            block = s.leaving.at[span(source * half, half)]

            @pl.when(source != me)
            def _():
                send(block, into, s.row_sent.at[source], s.row_came.at[me], (source, core))

            @pl.when(source == me)
            def _():
                s.arrived[core, span(me * half, half), :] = picked[j * half : (j + 1) * half]

    over(tiles, serve)
    swap(1, s.reqs.at[core], s.reqs.at[core])

    for load in loads[1:]:
        load.wait()
    s.w_out[core] = staged[1][...].astype(LOWF)
    swap(2, s.w_out.at[core], s.w_out.at[core])
    ups = hidden // width
    for c in range(ups):
        s.w_up[core, :, c * width : (c + 1) * width] = staged[2 + c][...].astype(LOWF)
    swap(3, s.w_up.at[core], s.w_up.at[core])
    s.w_down[core] = staged[2 + ups][...].astype(LOWF)
    swap(4, s.w_down.at[core], s.w_down.at[core])
    for c in range(3):
        s.w_in[c] = staged[3 + ups + c][...].astype(LOWF)
    high = staged[-1][...].astype(LOWF)
    s.pos_high[...] = high
    s.pos_low[...] = (staged[-1][...] - high.astype(WIDE)).astype(LOWF)
    seg = seg_ref[...]
    level = tile_iota((LEVELS, slots), 0)
    starts = jnp.sum(jnp.where(seg < level, 1.0, 0.0), 1, keepdims=True)
    start = jnp.sum(jnp.where(seg == level, starts, 0.0), 0, keepdims=True)
    place_row = tile_iota((1, slots), 1) - start.astype(jnp.int32)
    s.place_row[...] = place_row
    seg_wide = seg.astype(WIDE)
    for b in range(slots // TILE):
        at = slice(b * TILE, (b + 1) * TILE)
        s.segments[at, :] = as_column(seg_wide[:, at], eye, ones)
        s.place[at, :] = column_of(place_row[:, at])
    found, _ = windows(slots)
    causal = tile_iota((TILE, TILE), 0) <= tile_iota((TILE, TILE), 1)
    for b, low, wide, at in found:
        line = seg_wide[:, b * TILE : (b + 1) * TILE]
        for t in range(wide // TILE):
            same = s.segments[low + t * TILE : low + (t + 1) * TILE, :] == line
            if low + t * TILE == b * TILE:
                same = same & causal
            s.bias[at + t * TILE : at + (t + 1) * TILE, :] = jnp.where(same, 0.0, LOWEST)
    live = live_ref[0]
    alive_row = tile_iota((1, slots), 1) < live
    s.logit_bias[...] = jnp.where(alive_row, -logq_ref[...], LOWEST)
    first_lanes = (tile_iota((1, TILE), 1) < HEAD).astype(WIDE)
    pick = [first_lanes.astype(LOWF), (1.0 - first_lanes).astype(LOWF)]
    gain = [gain_ref[g : g + 1, :] for g in range(3)]
    step = 2 * TILE

    def group_at(k):
        near = spans // 2
        turn = jnp.where(k < near // 2, k, jnp.where(k < near // 2 + near, k + near // 2, k - near))
        return flipped(me * half // GROUP, spans - 1 - turn, 3)

    def lay(side, group):
        came = s.arrived[side, span(group * GROUP, GROUP), :]
        base = (side * entries + group * GROUP).astype(WIDE)
        lane = tile_iota((GROUP, TILE), 1).astype(WIDE)

        def block(b):
            at = span(b * GROUP, GROUP)
            where = s.column[at, :] - base
            hot = jnp.concatenate([one_hot(where == lane), one_hot(where == lane + float(TILE))], 1)
            s.total[at, :] += matmul(hot, came)

        over(slots // GROUP, block)

    def take(k, buffer, came, sent_on, passed, use):
        group = group_at(k)
        for j in range(GROUP // half):
            owner = group * (GROUP // half) + j

            @pl.when(owner != me)
            def _():
                arrived(buffer.at[core, span(owner * half, half)], came.at[owner])

        block = buffer.at[core, span(group * GROUP, GROUP)]
        send(block, block, sent_on.at[group], passed.at[group], (me, other))
        use(core, group)

        @pl.when(k > 0)
        def _():
            last = group_at(k - 1)
            arrived(buffer.at[other, span(last * GROUP, GROUP)], passed.at[last])
            use(other, last)

    def take_all(buffer, came, sent_on, passed, use, between=None):
        def run(k):
            take(k, buffer, came, sent_on, passed, use)
            if between is not None:
                between(k)

        over(spans, run)
        last = group_at(jnp.int32(spans - 1))
        arrived(buffer.at[other, span(last * GROUP, GROUP)], passed.at[last])
        use(other, last)

    take_all(s.arrived, s.row_came, s.pass_sent, s.pass_came, lay)
    s.cands[mine, :] = s.total[own:, :].astype(LOWF)
    swap(5, s.cands.at[mine], s.cands.at[mine])

    def enter(r):
        at = span(r * step, step)
        full = span(core * own + r * step, step, TILE)
        where = s.place[full, :]
        lane = tile_iota((step, TILE), 1).astype(WIDE)
        hot = jnp.concatenate(
            [one_hot(where == lane + float(t * TILE)) for t in range(places // TILE)], 1
        )
        first = s.total[at, :] + matmul(hot, s.pos_high[...]) + matmul(hot, s.pos_low[...])
        s.first[at, :] = first
        unit, inverse = spread_rows(first)
        s.unit_zero[at, :] = unit
        s.inverse_zero[at, :] = jnp.broadcast_to(inverse, (step, TILE))
        s.normed[full, :] = (unit * gain[0]).astype(LOWF)

    over(own // step, enter)
    swap(6, s.normed.at[mine], s.normed.at[mine])

    def project(k):
        @pl.when(k == own // step)
        def _():
            swapped(6, s.normed.at[yours])

        block = (core * (own // step) + k) % (slots // step)
        full = span(block * step, step, TILE)
        normed = s.normed[full, :]
        s.normed_t[:, full] = normed.astype(WIDE).T.astype(LOWF)
        query = (matmul(normed, s.w_in[0]) * SCALE).astype(LOWF)
        keys = matmul(normed, s.w_in[1]).astype(LOWF)
        values = matmul(normed, s.w_in[2]).astype(LOWF)
        keys_t = keys.astype(WIDE).T.astype(LOWF)
        values_t = values.astype(WIDE).T.astype(LOWF)
        for hp in range(pairs):
            lanes = slice(hp * TILE, (hp + 1) * TILE)
            s.keys[hp, full, :] = keys[:, lanes]
            s.values[hp, full, :] = values[:, lanes]
            s.keys_t[hp, :, full] = keys_t[lanes, :]
            s.values_t[hp, :, full] = values_t[lanes, :]
            for i in range(step // TILE):
                part = query[i * TILE : (i + 1) * TILE, lanes]
                for h in range(2):
                    s.queries[hp, block * (step // TILE) + i, h * TILE : (h + 1) * TILE, :] = (
                        part * pick[h]
                    )

    over(slots // step, project)

    def attend(hp):
        for b, low, wide, at in found:
            scores = matmul(s.keys[hp, low : low + wide, :], s.queries[hp, b], NT)
            bias = s.bias[at : at + wide, :]
            scores = scores + jnp.concatenate([bias, bias], 1)
            expo = jnp.exp(scores - jnp.max(scores, 0, keepdims=True))
            prob = expo * (1.0 / jnp.sum(expo, 0, keepdims=True))
            s.probs[hp, at : at + wide, :] = prob
            out = matmul(s.values_t[hp, :, low : low + wide], prob.astype(LOWF))
            out = jnp.concatenate([out[:HEAD, :TILE], out[HEAD:, TILE:]], 0)
            s.mixed[hp, b * TILE : (b + 1) * TILE, :] = out.T.astype(LOWF)
        swap(7 + hp, s.mixed.at[hp, yours], s.mixed_in.at[hp])

    over(pairs, attend)
    for index, block in enumerate((s.w_out, s.w_up, s.w_down)):
        swapped(2 + index, block.at[other])
    for hp in range(pairs):
        swapped(7 + hp, s.mixed_in.at[hp])

    def slopes(side, q, r):
        buffer = (s.d_keys, s.d_values)[side]
        fold = slots // own
        return buffer.at[q // fold, span(q % fold * own + r * step, step)]

    def feed(r):
        at = span(r * step, step)
        full = span(core * own + r * step, step, TILE)
        here = jnp.concatenate([s.mixed[hp, full, :] for hp in range(pairs)], 1)
        there = jnp.concatenate([s.mixed_in[hp, at, :] for hp in range(pairs)], 1)
        s.joined[core, at, :] = here
        s.joined[other, at, :] = there
        second = s.first[at, :] + matmul(here, s.w_out[core]) + matmul(there, s.w_out[other])
        unit, inverse = spread_rows(second)
        s.unit_one[at, :] = unit
        s.inverse_one[at, :] = jnp.broadcast_to(inverse, (step, TILE))
        lifted = (unit * gain[1]).astype(LOWF)
        s.lifted[at, :] = lifted
        third = second
        for side in range(2):
            inner = matmul(lifted, s.w_up[side])
            square = inner * inner
            bend = jnp.tanh(GELU_A * inner * (1.0 + GELU_B * square))
            gate = 0.5 * (1.0 + bend)
            act = (inner * gate).astype(LOWF)
            s.hidden[side, at, :] = act
            slope = gate + 0.5 * inner * (1.0 - bend * bend) * (
                GELU_A * (1.0 + 3.0 * GELU_B * square)
            )
            for q in range(hidden // TILE):
                slopes(side, q, r)[...] = slope[:, q * TILE : (q + 1) * TILE]
            third = third + matmul(act, s.w_down[side])
        unit, inverse = spread_rows(third)
        s.unit_two[at, :] = unit
        s.inverse_two[at, :] = jnp.broadcast_to(inverse, (step, TILE))
        s.final[at, :] = (unit * gain[2]).astype(LOWF)

    over(own // step, feed)
    s.few[...] = jnp.zeros((8, width), WIDE)
    swapped(5, s.cands.at[yours])

    def choose(r):
        at = span(r * TILE, TILE)
        logits = matmul(s.final[at, :], s.cands[...], NT) + s.logit_bias[...]
        number = tile_iota((TILE, slots), 0) + (core * own + r * TILE)
        same = tile_iota((TILE, slots), 1) == number
        top = jnp.max(logits, -1, keepdims=True)
        expo = jnp.exp(logits - top)
        total = jnp.sum(expo, -1, keepdims=True)
        alive = number[:, :1] < live
        right = jnp.sum(jnp.where(same, logits, 0.0), -1, keepdims=True)
        loss = jnp.sum(jnp.where(alive, top + jnp.log(total) - right, 0.0))
        s.few[3:4, :] += jnp.full((1, width), loss, WIDE)
        alive = jnp.where(alive, 1.0, 0.0)
        grad = (expo * (alive / total) - jnp.where(same, alive, 0.0)).astype(LOWF)
        s.d_logits[at, :] = grad
        d_final = matmul(grad, s.cands[...])
        unit = s.unit_two[at, :]
        s.few[2:3, :] += jnp.sum(d_final * unit, 0, keepdims=True)
        d_third = spread_back(unit, s.inverse_two[at, :1], gain[2], d_final)
        s.d_third[at, :] = d_third
        s.d_branch[at, :] = d_third.astype(LOWF)

    over(own // TILE, choose)

    def feed_back(r):
        at = span(r * step, step)
        full = span(core * own + r * step, step, TILE)
        d_lifted = jnp.zeros((step, width), WIDE)
        for side in range(2):
            d_hidden = matmul(s.d_branch[at, :], s.w_down[side], NT)
            slope = jnp.concatenate([slopes(side, q, r)[...] for q in range(hidden // TILE)], 1)
            d_inner = (d_hidden * slope).astype(LOWF)
            s.d_inner[side, at, :] = d_inner
            d_lifted = d_lifted + matmul(d_inner, s.w_up[side], NT)
        unit = s.unit_one[at, :]
        s.few[1:2, :] += jnp.sum(d_lifted * unit, 0, keepdims=True)
        d_second = s.d_third[at, :] + spread_back(unit, s.inverse_one[at, :1], gain[1], d_lifted)
        s.d_second[at, :] = d_second
        d_mixed = d_second.astype(LOWF)
        s.d_mixed[at, :] = d_mixed
        here = matmul(d_mixed, s.w_out[core], NT).astype(LOWF)
        there = matmul(d_mixed, s.w_out[other], NT).astype(LOWF)
        for hp in range(pairs):
            lanes = slice(hp * TILE, (hp + 1) * TILE)
            s.d_heads[hp, full, :] = here[:, lanes]
            s.d_heads_out[hp, at, :] = there[:, lanes]

    over(own // step, feed_back)
    for hp in range(pairs):
        swap(9 + hp, s.d_heads_out.at[hp], s.d_heads.at[hp, mine])
    for side in range(2):
        s.g_down[side] = matmul(s.hidden[side], s.d_branch[...], TN)
    swap(11, s.g_down.at[other], s.g_down_in)
    for side in range(2):
        s.g_up[side] = matmul(s.lifted[...], s.d_inner[side], TN)
    swap(12, s.g_up.at[other], s.g_up_in)
    for side in range(2):
        s.g_out[side] = matmul(s.joined[side], s.d_mixed[...], TN)
    swap(13, s.g_out.at[other], s.g_out_in)
    d_cand = matmul(s.d_logits[...], s.final[...], TN)
    for c in range(width // TILE):
        s.d_cand[c * slots : (c + 1) * slots, :] = d_cand[:, c * TILE : (c + 1) * TILE]
    swap(14, s.d_cand, s.d_cand_in)
    s.d_keys[...] = jnp.zeros(s.d_keys.shape, WIDE)
    s.d_values[...] = jnp.zeros(s.d_values.shape, WIDE)

    def give_early():
        swapped(11, s.g_down_in)
        swapped(12, s.g_up_in)
        swapped(13, s.g_out_in)
        g_up = s.g_up[core] + s.g_up_in[...]
        at = 0
        for block in (
            s.g_out[core] + s.g_out_in[...],
            *(g_up[:, c * width : (c + 1) * width] for c in range(hidden // width)),
            s.g_down[core] + s.g_down_in[...],
        ):
            early.source[at : at + block.shape[0], :] = block.astype(LOWF)
            at += block.shape[0]
        if at < early.source.shape[0]:
            early.source[at:, :] = jnp.zeros((early.source.shape[0] - at, width), LOWF)
        early.start()

    give_early()
    for hp in range(pairs):
        swapped(9 + hp, s.d_heads.at[hp, yours])

    def attend_back(hp):
        for b, low, wide, at in found:
            d_block = s.d_heads[hp, b * TILE : (b + 1) * TILE, :]
            d_pair = jnp.concatenate([d_block * pick[0], d_block * pick[1]], 0)
            d_prob = matmul(s.values[hp, low : low + wide, :], d_pair, NT)
            prob = s.probs[hp, at : at + wide, :]
            mean = jnp.sum(prob * d_prob, 0, keepdims=True)
            d_scores = (prob * (d_prob - mean)).astype(LOWF)
            s.d_keys[hp, low : low + wide, :] += matmul(d_scores, s.queries[hp, b])
            s.d_values[hp, low : low + wide, :] += matmul(prob.astype(LOWF), d_pair)
            out = matmul(s.keys_t[hp, :, low : low + wide], d_scores)
            out = jnp.concatenate([out[:HEAD, :TILE], out[HEAD:, TILE:]], 0) * SCALE
            lanes = span(hp * TILE, TILE, TILE)
            s.d_triple[0, b * TILE : (b + 1) * TILE, lanes] = out.T.astype(LOWF)

        @pl.when(hp == pairs - 1)
        def _():
            early.across()

    over(pairs, attend_back)
    for hp in range(pairs):
        lanes = slice(hp * TILE, (hp + 1) * TILE)
        s.d_triple[1, :, lanes] = s.d_keys[hp].astype(LOWF)
        s.d_triple[2, :, lanes] = s.d_values[hp].astype(LOWF)
    for side in (yours, mine):
        d_normed = matmul(s.d_triple[0, side, :], s.w_in[0], NT)
        for c in range(1, 3):
            d_normed = d_normed + matmul(s.d_triple[c, side, :], s.w_in[c], NT)
        s.d_normed[side, :] = d_normed
        if side is yours:
            swap(15, s.d_normed.at[yours], s.d_normed_in)
    swapped(15, s.d_normed_in)
    d_normed = s.d_normed[mine, :] + s.d_normed_in[...]
    unit = s.unit_zero[...]
    s.few[0:1, :] = jnp.sum(d_normed * unit, 0, keepdims=True)
    d_first = s.d_second[...] + spread_back(unit, s.inverse_zero[:, :1], gain[0], d_normed)
    s.d_rows[mine, :] = d_first.astype(LOWF)
    swap(16, s.d_rows.at[mine], s.d_rows.at[mine])
    s.few[4:5, :] = jnp.full((1, width), 0.5 * live.astype(WIDE), WIDE)
    swap(17, s.few, s.few_in)
    swapped(14, s.d_cand_in)
    for c in range(width // TILE):
        at = pl.ds(c * slots, slots)
        s.d_rows[slots:, c * TILE : (c + 1) * TILE] = (s.d_cand[at, :] + s.d_cand_in[at, :]).astype(LOWF)
    for c in range(3):
        late.source[c * width : (c + 1) * width, :] = matmul(s.normed_t[...], s.d_triple[c]).astype(LOWF)
    pos_at = 3 * width
    pos_half = places // 2
    swapped(16, s.d_rows.at[yours])
    hot = one_hot(tile_iota((pos_half, slots), 0) + core * pos_half == s.place_row[...])
    late.source[pos_at : pos_at + pos_half, :] = matmul(hot, s.d_rows[:slots, :]).astype(LOWF)
    if pos_at + pos_half < late.source.shape[0]:
        late.source[pos_at + pos_half :, :] = jnp.zeros(
            (late.source.shape[0] - pos_at - pos_half, width), LOWF
        )
    late.start()
    swapped(17, s.few_in)
    s.few_all[me] = s.few[...] + s.few_in[...]

    def give_few(k):
        where = (me + k + 1) % groups
        send(s.few_all.at[me], s.few_all.at[me], s.few_sent.at[where], s.few_came.at[me], (where, core))

    over(groups - 1, give_few)
    early.settle()

    over(
        groups - 1,
        lambda k: departed(
            s.leaving.at[span((me + k + 1) % groups * half, half)], s.row_sent.at[(me + k + 1) % groups]
        ),
    )

    def give_rows(k):
        tile = flipped(me // share, tiles - 1 - k)
        number = s.flat[...] - (core * entries + tile * TILE)
        hot = one_hot(tile_iota((TILE, entries), 0) == number)
        picked = matmul(hot, s.d_rows[...]).astype(LOWF)
        s.leaving[span(tile * TILE, TILE), :] = picked
        into = s.landed.at[core, span(me * half, half)]
        for j in range(share):
            owner = tile * share + j
            block = s.leaving.at[span(owner * half, half)]

            @pl.when(owner != me)
            def _():
                send(block, into, s.land_sent.at[owner], s.land_came.at[me], (owner, core))

            @pl.when(owner == me)
            def _():
                s.landed[core, span(me * half, half), :] = picked[j * half : (j + 1) * half]

    over(tiles, give_rows)
    late.across()
    early.forward()
    late.settle()
    swapped(1, s.reqs.at[other])
    s.grad_table[...] = jnp.zeros(s.grad_table.shape, WIDE)
    part = held // 7

    def gather(side, group):
        came = s.landed[side, span(group * GROUP, GROUP), :]
        first_row = core * held + 1
        lines = [s.reqs[side, pl.ds(2 * group + i, 1), :] - first_row for i in range(2)]

        def block(b):
            at = span(b * part, part, 8)
            rows = tile_iota((part, TILE), 0) + b * part
            hot = jnp.concatenate([one_hot(rows == line) for line in lines], 1)
            s.grad_table[at, :] += matmul(hot, came)

        over(7, block)

    def between(k):
        @pl.when(k == spans // 2)
        def _():
            late.forward()

    take_all(s.landed, s.land_came, s.hand_sent, s.hand_came, gather, between)
    final = s.grad_table[...]
    table_ref[...] = final
    square = (
        jnp.sum(final * final)
        + jnp.sum(early.shard[...] * early.shard[...])
        + jnp.sum(late.shard[...] * late.shard[...])
    )
    s.squares[slot_of] = jnp.full((8, TILE), square, WIDE)

    def square_copy(k):
        where = (slot_of + k + 1) % (2 * groups)
        block = s.squares.at[slot_of]
        return copy_to(
            block, block, s.square_sent.at[where], s.square_came.at[slot_of], (where // 2, where % 2)
        )

    over(2 * groups - 1, lambda k: square_copy(k).start())
    late.collect()
    position_own = s.late_whole.at[pos_at : pos_at + pos_half]
    swap(18, position_own, s.other_half)
    early.collect()
    early_ref[...] = s.early_whole[: early_ref.shape[0], :]
    late_ref[...] = s.late_whole[: late_ref.shape[0], :]

    def take_few(k):
        where = (me + k + 1) % groups
        arrived(s.few_all.at[where], s.few_came.at[where])

    over(groups - 1, take_few)
    few_total = s.few_all[0]
    for source in range(1, groups):
        few_total = few_total + s.few_all[source]
    few_ref[...] = few_total
    position_ref[span(core * pos_half, pos_half), :] = s.late_whole[pos_at : pos_at + pos_half, :]
    swapped(18, s.other_half)
    position_ref[span(other * pos_half, pos_half), :] = s.other_half[...]

    def take_square(k):
        where = (slot_of + k + 1) % (2 * groups)
        arrived(s.squares.at[where], s.square_came.at[where])

    over(2 * groups - 1, take_square)
    gains = few_total[:3]
    norm = jnp.sqrt(jnp.sum(s.squares[...], 0) + jnp.sum(gains * gains))
    stats_ref[...] = norm

    early.drain()
    late.drain()

    def finish(k):
        where = (me + k + 1) % groups
        departed(s.want.at[where], s.want_sent.at[where])
        departed(s.leaving.at[span(where * half, half)], s.land_sent.at[where])
        departed(s.few_all.at[me], s.few_sent.at[where])

    over(groups - 1, finish)

    def finish_group(group):
        block = s.arrived.at[core, span(group * GROUP, GROUP)]
        departed(block, s.pass_sent.at[group])
        departed(block, s.hand_sent.at[group])

    over(spans, finish_group)
    over(2 * groups - 1, lambda k: square_copy(k).wait_send())
    ends = [s.table.at[rows_mine], s.reqs.at[core], s.w_out.at[core], s.w_up.at[core], s.w_down.at[core]]
    ends += [s.cands.at[mine], s.normed.at[mine]]
    ends += [s.mixed.at[hp, yours] for hp in range(2)] + [s.d_heads_out.at[hp] for hp in range(2)]
    ends += [s.g_down.at[other], s.g_up.at[other], s.g_out.at[other], s.d_cand, s.d_normed.at[yours]]
    ends += [s.d_rows.at[mine], s.few, position_own]
    for index, ref in enumerate(ends):
        departed(ref, s.sent.at[index])


def run_step(table, attn_in, attn_out, ffn_up, ffn_down, position, owners, offsets, seg, live, logq, gains, groups):
    held, width = table.shape
    entries = owners.shape[1]
    heads_width, hidden, places = attn_out.shape[0], ffn_up.shape[1], position.shape[0]
    scratch = step_scratch(groups, held, entries, width, heads_width, hidden, places)
    shape = jax.ShapeDtypeStruct
    return pl.pallas_call(
        functools.partial(step_kernel, groups, tuple(scratch)),
        out_shape=(
            shape((held, width), WIDE),
            shape((heads_width + 2 * hidden, width), LOWF),
            shape((3 * heads_width, width), LOWF),
            shape((places, width), LOWF),
            shape((8, width), WIDE),
            shape((8, TILE), WIDE),
        ),
        in_specs=[FAR] * 6 + [VMEM] * 3 + [SMEM] + [VMEM] * 2,
        out_specs=(VMEM,) * 6,
        scratch_shapes=list(scratch.values()),
        compiler_params=pltpu.CompilerParams(
            collective_id=0, has_side_effects=True, vmem_limit_bytes=60 * 1024 * 1024
        ),
    )(table, attn_in, attn_out, ffn_up, ffn_down, position, owners, offsets, seg, live, logq, gains)


def adamw(weight, grad, first, second, decay, rate):
    first = BETA_ONE * first + (1.0 - BETA_ONE) * grad
    second = BETA_TWO * second + (1.0 - BETA_TWO) * grad * grad
    moved = first / (1.0 - BETA_ONE**STEP) / (jnp.sqrt(second / (1.0 - BETA_TWO**STEP)) + ADAM_EPS)
    return (weight - rate * (moved + decay * weight), first, second)


def update_kernel(table_g, early_g, late_g, position_g, few_ref, stats_ref, *refs):
    inputs, outputs, buffers = refs[:21], refs[21:45], refs[45:63]
    came, left = refs[63], refs[64]
    names = ("table", "in", "out", "up", "down", "position")
    ins = [pltpu.make_async_copy(inputs[i], buffers[i], came.at[i]) for i in range(18)]
    outs = [pltpu.make_async_copy(buffers[i], outputs[i], left.at[i]) for i in range(18)]
    for copy in ins:
        copy.start()
    norm = stats_ref[0, 0]
    factor = CLIP / jnp.maximum(norm, CLIP)
    gains = adamw(
        inputs[18][...], few_ref[0:3, :] * factor, inputs[19][...], inputs[20][...], 0.0, RATE_GAINS
    )
    for ref, value in zip(outputs[18:21], gains):
        ref[...] = value
    outputs[21][0, 0] = few_ref[3, 0]
    outputs[22][0, 0] = few_ref[4, 0]
    outputs[23][0, 0] = norm
    width = table_g.shape[1]
    block = 16
    for index, name in enumerate(names):
        trio = buffers[3 * index : 3 * index + 3]
        for i in range(3):
            ins[3 * index + i].wait()
        rate = RATE_POSITION if name == "position" else RATE
        lead = trio[0].shape[0] if name == "in" else 1
        rows, columns = trio[0].shape[-2:]
        heads_width, hidden = buffers[6].shape[0], buffers[9].shape[1]

        def run(r, index=index, name=name, trio=trio, rows=rows, rate=rate):
            at = span(r * block, block)
            views = [ref.at[r * block // rows, span(r * block % rows, block)] if name == "in" else ref.at[at] for ref in trio]
            if name == "table":
                grad = table_g[at, :]
            elif name == "in":
                grad = late_g[at, :].astype(WIDE)
            elif name == "out":
                grad = early_g[at, :].astype(WIDE)
            elif name == "up":
                grad = jnp.concatenate(
                    [
                        early_g[span(heads_width + c * width + r * block, block), :].astype(WIDE)
                        for c in range(hidden // width)
                    ],
                    1,
                )
            elif name == "down":
                grad = early_g[span(heads_width + hidden + r * block, block), :].astype(WIDE)
            else:
                grad = position_g[at, :].astype(WIDE)
            made = adamw(views[0][...], grad * factor, views[1][...], views[2][...], DECAY, rate)
            for view, value in zip(views, made):
                view[...] = value

        over(lead * rows // block, run)
        for i in range(3):
            outs[3 * index + i].start()
    for copy in outs:
        copy.wait()


def run_update(grads, trios):
    flat = [array for trio in trios for array in trio]
    shape = jax.ShapeDtypeStruct
    scalar = shape((1, 1), WIDE)
    return pl.pallas_call(
        update_kernel,
        out_shape=tuple(shape(a.shape, WIDE) for a in flat) + (scalar,) * 3,
        in_specs=[VMEM] * 5 + [VMEM] + [FAR] * 18 + [VMEM] * 3,
        out_specs=(FAR,) * 18 + (VMEM,) * 3 + (SMEM,) * 3,
        scratch_shapes=[pltpu.VMEM(a.shape, WIDE) for a in flat[:18]] + [DMA((18,)), DMA((18,))],
        compiler_params=pltpu.CompilerParams(vmem_limit_bytes=60 * 1024 * 1024),
    )(*grads, *flat)


def body(
    item_table,
    attn_in,
    attn_out,
    ffn_up,
    ffn_down,
    position_table,
    norm_gains,
    item_first,
    item_second,
    attn_in_first,
    attn_in_second,
    attn_out_first,
    attn_out_second,
    ffn_up_first,
    ffn_up_second,
    ffn_down_first,
    ffn_down_second,
    position_first,
    position_second,
    gains_first,
    gains_second,
    owner_group,
    row_offset,
    segment_ids,
    live_slots,
    log_freq,
):
    grads = run_step(
        item_table,
        attn_in,
        attn_out,
        ffn_up,
        ffn_down,
        position_table,
        owner_group.reshape(1, -1),
        row_offset,
        segment_ids,
        live_slots,
        log_freq,
        norm_gains,
        lax.axis_size("dp"),
    )
    made = run_update(
        grads,
        (
            (item_table, item_first, item_second),
            (attn_in, attn_in_first, attn_in_second),
            (attn_out, attn_out_first, attn_out_second),
            (ffn_up, ffn_up_first, ffn_up_second),
            (ffn_down, ffn_down_first, ffn_down_second),
            (position_table, position_first, position_second),
            (norm_gains, gains_first, gains_second),
        ),
    )
    return (*made[:21], *(scalar.reshape(()) for scalar in made[21:]))


def solution(mesh):
    return jax.shard_map(
        body,
        mesh=mesh,
        in_specs=(
            P(("dp", "ffn"), None),
            P(None, None, "ffn"),
            P("ffn", None),
            P(None, "ffn"),
            P("ffn", None),
            P(),
            P(),
            P(("dp", "ffn"), None),
            P(("dp", "ffn"), None),
            P(None, None, "ffn"),
            P(None, None, "ffn"),
            P("ffn", None),
            P("ffn", None),
            P(None, "ffn"),
            P(None, "ffn"),
            P("ffn", None),
            P("ffn", None),
            P(),
            P(),
            P(),
            P(),
            P("dp", None, None),
            P("dp", None),
            P("dp", None),
            P("dp"),
            P("dp", None),
        ),
        out_specs=(
            P(("dp", "ffn"), None),
            P(("dp", "ffn"), None),
            P(("dp", "ffn"), None),
            P(None, None, "ffn"),
            P(None, None, "ffn"),
            P(None, None, "ffn"),
            P("ffn", None),
            P("ffn", None),
            P("ffn", None),
            P(None, "ffn"),
            P(None, "ffn"),
            P(None, "ffn"),
            P("ffn", None),
            P("ffn", None),
            P("ffn", None),
            P(),
            P(),
            P(),
            P(),
            P(),
            P(),
            P(),
            P(),
            P(),
        ),
        check_vma=False,
    )
```

time: 691 us -> 157 us (0.23)
  blocking collectives: 183 us -> 0 us
  waiting for transfers between devices: 181 us -> 0 us
  Pallas kernels: 0 us -> 155 us
  other arithmetic: 123 us -> 0 us
  local copies, waits for them, and re-layouts: 101 us -> 0 us
  matrix products: 59.1 us -> 0 us
  between operations: 22.4 us -> 1.47 us
  starting transfers between devices: 16.2 us -> 0 us
    psum x6 -> x0, waiting for transfers between devices: 174 us -> none  [the longest x1 82.5 us: body(): lax.psum((grads[0], grads[1], grads[2], grads[3], grads[4], grads[5], los...]
    pallas_call x0 -> x2, Pallas kernels: none -> 155 us  [the longest x1 144 us: run_step(): pl.pallas_call(functools.partial(step_kernel, groups, tuple(scratch)), ou...]
    psum x2 -> x0, blocking collectives: 132 us -> none  [the longest x1 92.8 us: body(): lax.psum((grads[0], grads[1], grads[2], grads[3], grads[4], grads[5], los...]
    gather x4 -> x0, local copies, waits for them, and re-layouts: 70.3 us -> none  [the longest x1 35 us: fetch_rows(): return (whole[owners, ranks], local)]
    dot_general x27 -> x0, matrix products: 59.1 us -> none  [the longest x2 12 us: attend_back(): jnp.einsum('qhe,khe->hqk', d_part, values, preferred_element_type=WIDE)]
    all_to_all x1 -> x0, blocking collectives: 51.2 us -> none  [fetch_rows(): lax.all_to_all(picked, 'dp', split_axis=0, concat_axis=0, tiled=True)]
    scatter-add x2 -> x0, other arithmetic: 34.2 us -> none  [the longest x1 26.8 us: body(): grad_table = jnp.zeros(item_table.shape, WIDE).at[jnp.clip(served_now, 0,...]
    reduce_sum x20 -> x0, other arithmetic: 25.3 us -> none  [the longest x2 3.79 us: norm_back(): return (d_value, jnp.sum(grad * unit, 0))]
  transfers between devices with their start and end apart: 8 -> 0, of which waited for: 7 -> 0; matrix products, arithmetic and copies ran while one was open for 8% -> 0% of each run, Pallas kernels for 0% -> 0%
where the time goes in v1:
time: 157 us
  Pallas kernels  155 us (99%)
    pallas_call x1, Pallas kernels, run_step(): pl.pallas_call(functools.partial(step_kernel, groups, tuple(scratch)), ou...  144 us
    pallas_call x1, Pallas kernels, run_update(): pl.pallas_call(update_kernel, out_shape=tuple((shape(a.shape, WIDE) for a...  11.2 us

profile of v1, /device:TPU:0, one launch (start us, length us, event | category | flops | bytes accessed | tf_op | source)
XLA Modules:
  0.0 156.6 jit_solution(5442937775297849249)
XLA Ops:
  1.3 143.9 %shard_map.433 = (f32[784,256]{1,0:T(8,128)}, bf16[1280,256]{1,0:T(8,128)(2,1)}, bf16[768,256]{1,0:T(8,128)(2,1)}, bf16[512,256]{1,0:T(8,128)(2,1)}, f32[8,256]{1,0:T(8,128)}, /*index=5*/f32[8,128]{1,0:T(8,128)}) custom-call(f32[784,256]{1,0:T(8,128)} %refs_0_.3, f32[3,256,256]{2,1,0:T(8,128)} %refs_3_.3, f32[256,256]{1,0:T(8,128)} %refs_6_.1, ...), custom_call_target="tpu_custom_call" | custom-call | tf_op jit(solution)/shard_map/pallas_call | solution.py:1002
  145.2 11.2 %shard_map.434 = (f32[784,256]{1,0:T(8,128)}, f32[784,256]{1,0:T(8,128)}, f32[784,256]{1,0:T(8,128)}, f32[3,256,256]{2,1,0:T(8,128)}, f32[3,256,256]{2,1,0:T(8,1...) custom-call(f32[784,256]{1,0:T(8,128)} %get-tuple-element.54.table_g, ...), custom_call_target="tpu_custom_call" | custom-call | tf_op jit(solution)/shard_map/pallas_call | solution.py:1093

commit v2 on v1

--- a/solution.py
+++ b/solution.py
@@ -265,7 +265,6 @@
     shapes = {
         "table": ((padded, width), LOWF),
         "flat": ((1, entries), jnp.int32),
-        "column": ((slots, TILE), WIDE),
         "want": ((groups, 8, TILE), jnp.int32),
         "asked": ((groups, 8, TILE), jnp.int32),
         "reqs": ((2, entries // TILE, TILE), jnp.int32),
@@ -276,8 +275,6 @@
         "w_up": ((2, width, hidden), LOWF),
         "w_down": ((2, hidden, width), LOWF),
         "w_in": ((3, width, heads_width), LOWF),
-        "segments": ((slots, TILE), WIDE),
-        "place": ((slots, TILE), WIDE),
         "place_row": ((1, slots), jnp.int32),
         "bias": ((area, TILE), WIDE),
         "pos_high": ((places, width), LOWF),
@@ -313,12 +310,15 @@
         "d_heads": ((pairs, slots, TILE), LOWF),
         "d_heads_out": ((pairs, own, TILE), LOWF),
         "d_cand": ((slots * width // TILE, TILE), WIDE),
-        "g_out": ((2, heads_width, width), WIDE),
-        "g_up": ((2, width, hidden), WIDE),
-        "g_down": ((2, hidden, width), WIDE),
-        "g_out_in": ((heads_width, width), WIDE),
-        "g_up_in": ((width, hidden), WIDE),
-        "g_down_in": ((hidden, width), WIDE),
+        "g_out": ((heads_width, width), WIDE),
+        "g_up": ((width, hidden), WIDE),
+        "g_down": ((hidden, width), WIDE),
+        "g_out_out": ((heads_width, width), LOWF),
+        "g_up_out": ((width, hidden), LOWF),
+        "g_down_out": ((hidden, width), LOWF),
+        "g_out_in": ((heads_width, width), LOWF),
+        "g_up_in": ((width, hidden), LOWF),
+        "g_down_in": ((hidden, width), LOWF),
         "d_keys": ((pairs, slots, TILE), WIDE),
         "d_values": ((pairs, slots, TILE), WIDE),
         "d_triple": ((3, slots, heads_width), LOWF),
@@ -327,7 +327,6 @@
         "few": ((8, width), WIDE),
         "few_in": ((8, width), WIDE),
         "few_all": ((groups, 8, width), WIDE),
-        "landed": ((2, entries, width), LOWF),
         "squares": ((2 * groups, 8, TILE), WIDE),
         "early_whole": ((groups * shard_rows(2 * hidden + heads_width, groups), width), LOWF),
         "late_whole": ((groups * shard_rows(3 * heads_width + places // 2, groups), width), LOWF),
@@ -344,17 +343,20 @@
     scratch["square_came"] = DMA((2 * groups,))
     scratch["sent"] = DMA((LINKS,))
     scratch["came"] = DMA((LINKS,))
-    scratch["loads"] = DMA((12,))
+    scratch["loads"] = DMA((24,))
     scratch.update(part_scratch("early", 2 * hidden + heads_width, width, groups))
     scratch.update(part_scratch("late", 3 * heads_width + places // 2, width, groups))
     return scratch
 
 
-def step_kernel(groups, names, *refs):
-    (table_far, in_far, out_far, up_far, down_far, pos_far) = refs[:6]
-    (own_ref, off_ref, seg_ref, live_ref, logq_ref, gain_ref) = refs[6:12]
-    (table_ref, early_ref, late_ref, position_ref, few_ref, stats_ref) = refs[12:18]
-    s = types.SimpleNamespace(**dict(zip(names, refs[18:])))
+def step_kernel(groups, keeps, names, *refs):
+    (own_ref, off_ref, seg_ref, live_ref, logq_ref, gain_ref) = refs[:6]
+    count = 18 if keeps else 6
+    fars, refs = refs[6 : 6 + count], refs[6 + count :]
+    table_far, in_far, out_far, up_far, down_far, pos_far = fars[:: count // 6]
+    (table_ref, early_ref, late_ref, position_ref, few_ref, stats_ref) = refs[:6]
+    nears, refs = (refs[6:24], refs[24:]) if keeps else (None, refs[6:])
+    s = types.SimpleNamespace(**dict(zip(names, refs)))
     me, core = lax.axis_index("dp"), lax.axis_index("ffn")
     other = 1 - core
     held, width = table_far.shape
@@ -383,14 +385,21 @@
     over(2 * groups - 1, greet)
     spare = s.probs.at[0]
     s.d_cand_in = s.bias.at[pl.ds(0, slots * width // TILE)]
+    s.column = s.probs.at[1, pl.ds(slots, slots), pl.ds(0, TILE)]
+    s.segments = s.probs.at[1, pl.ds(slots, slots), pl.ds(TILE, TILE)]
+    s.place = s.probs.at[1, pl.ds(2 * slots, slots), pl.ds(0, TILE)]
     s.total = s.d_normed = s.probs.at[1, pl.ds(0, slots)]
     s.grad_table = spare.at[pl.ds(0, held)]
     pieces = [table_far, out_far]
     pieces += [up_far.at[:, pl.ds(c * width, width)] for c in range(hidden // width)]
     pieces += [down_far, *(in_far.at[c] for c in range(3)), pos_far]
     loads, staged, at = [], [], 0
+    if keeps:
+        targets = [nears[0], nears[6]]
+        targets += [nears[9].at[:, pl.ds(c * width, width)] for c in range(hidden // width)]
+        targets += [nears[12], *(nears[3].at[c] for c in range(3)), nears[15]]
     for index, piece in enumerate(pieces):
-        near = spare.at[pl.ds(at, piece.shape[0])]
+        near = targets[index] if keeps else spare.at[pl.ds(at, piece.shape[0])]
         at += piece.shape[0]
         staged.append(near)
         loads.append(pltpu.make_async_copy(piece, near, s.loads.at[index]))
@@ -514,6 +523,12 @@
 
     for load in loads[1:]:
         load.wait()
+    keep = []
+    if keeps:
+        for i in range(12):
+            index = i // 2 * 3 + 1 + i % 2
+            keep.append(pltpu.make_async_copy(fars[index], nears[index], s.loads.at[12 + i]))
+            keep[-1].start()
     s.w_out[core] = staged[1][...].astype(LOWF)
     swap(2, s.w_out.at[core], s.w_out.at[core])
     ups = hidden // width
@@ -562,16 +577,10 @@
 
     def lay(side, group):
         came = s.arrived[side, span(group * GROUP, GROUP), :]
-        base = (side * entries + group * GROUP).astype(WIDE)
-        lane = tile_iota((GROUP, TILE), 1).astype(WIDE)
-
-        def block(b):
-            at = span(b * GROUP, GROUP)
-            where = s.column[at, :] - base
-            hot = jnp.concatenate([one_hot(where == lane), one_hot(where == lane + float(TILE))], 1)
-            s.total[at, :] += matmul(hot, came)
-
-        over(slots // GROUP, block)
+        where = s.column[...] - (side * entries + group * GROUP).astype(WIDE)
+        lane = tile_iota((slots, TILE), 1).astype(WIDE)
+        hot = jnp.concatenate([one_hot(where == lane), one_hot(where == lane + float(TILE))], 1)
+        s.total[...] += matmul(hot, came)
 
     def take(k, buffer, came, sent_on, passed, use):
         group = group_at(k)
@@ -670,6 +679,7 @@
     over(pairs, attend)
     for index, block in enumerate((s.w_out, s.w_up, s.w_down)):
         swapped(2 + index, block.at[other])
+    over(spans, lambda g: departed(s.arrived.at[core, span(g * GROUP, GROUP)], s.pass_sent.at[g]))
     for hp in range(pairs):
         swapped(7 + hp, s.mixed_in.at[hp])
 
@@ -737,6 +747,13 @@
         s.d_branch[at, :] = d_third.astype(LOWF)
 
     over(own // TILE, choose)
+    s.g_down_out[...] = matmul(s.hidden[other], s.d_branch[...], TN).astype(LOWF)
+    swap(11, s.g_down_out, s.g_down_in)
+    d_cand = matmul(s.d_logits[...], s.final[...], TN)
+    for c in range(width // TILE):
+        s.d_cand[c * slots : (c + 1) * slots, :] = d_cand[:, c * TILE : (c + 1) * TILE]
+    swap(14, s.d_cand, s.d_cand_in)
+    s.g_down[...] = matmul(s.hidden[core], s.d_branch[...], TN)
 
     def feed_back(r):
         at = span(r * step, step)
@@ -764,19 +781,12 @@
     over(own // step, feed_back)
     for hp in range(pairs):
         swap(9 + hp, s.d_heads_out.at[hp], s.d_heads.at[hp, mine])
-    for side in range(2):
-        s.g_down[side] = matmul(s.hidden[side], s.d_branch[...], TN)
-    swap(11, s.g_down.at[other], s.g_down_in)
-    for side in range(2):
-        s.g_up[side] = matmul(s.lifted[...], s.d_inner[side], TN)
-    swap(12, s.g_up.at[other], s.g_up_in)
-    for side in range(2):
-        s.g_out[side] = matmul(s.joined[side], s.d_mixed[...], TN)
-    swap(13, s.g_out.at[other], s.g_out_in)
-    d_cand = matmul(s.d_logits[...], s.final[...], TN)
-    for c in range(width // TILE):
-        s.d_cand[c * slots : (c + 1) * slots, :] = d_cand[:, c * TILE : (c + 1) * TILE]
-    swap(14, s.d_cand, s.d_cand_in)
+    s.g_up_out[...] = matmul(s.lifted[...], s.d_inner[other], TN).astype(LOWF)
+    swap(12, s.g_up_out, s.g_up_in)
+    s.g_out_out[...] = matmul(s.joined[other], s.d_mixed[...], TN).astype(LOWF)
+    swap(13, s.g_out_out, s.g_out_in)
+    s.g_up[...] = matmul(s.lifted[...], s.d_inner[core], TN)
+    s.g_out[...] = matmul(s.joined[core], s.d_mixed[...], TN)
     s.d_keys[...] = jnp.zeros(s.d_keys.shape, WIDE)
     s.d_values[...] = jnp.zeros(s.d_values.shape, WIDE)
 
@@ -784,12 +794,12 @@
         swapped(11, s.g_down_in)
         swapped(12, s.g_up_in)
         swapped(13, s.g_out_in)
-        g_up = s.g_up[core] + s.g_up_in[...]
+        g_up = s.g_up[...] + s.g_up_in[...].astype(WIDE)
         at = 0
         for block in (
-            s.g_out[core] + s.g_out_in[...],
+            s.g_out[...] + s.g_out_in[...].astype(WIDE),
             *(g_up[:, c * width : (c + 1) * width] for c in range(hidden // width)),
-            s.g_down[core] + s.g_down_in[...],
+            s.g_down[...] + s.g_down_in[...].astype(WIDE),
         ):
             early.source[at : at + block.shape[0], :] = block.astype(LOWF)
             at += block.shape[0]
@@ -797,7 +807,6 @@
             early.source[at:, :] = jnp.zeros((early.source.shape[0] - at, width), LOWF)
         early.start()
 
-    give_early()
     for hp in range(pairs):
         swapped(9 + hp, s.d_heads.at[hp, yours])
 
@@ -815,10 +824,9 @@
             out = jnp.concatenate([out[:HEAD, :TILE], out[HEAD:, TILE:]], 0) * SCALE
             lanes = span(hp * TILE, TILE, TILE)
             s.d_triple[0, b * TILE : (b + 1) * TILE, lanes] = out.T.astype(LOWF)
-
-        @pl.when(hp == pairs - 1)
-        def _():
-            early.across()
+            if b == 3:
+                pl.when(hp == 0)(give_early)
+
 
     over(pairs, attend_back)
     for hp in range(pairs):
@@ -832,24 +840,53 @@
         s.d_normed[side, :] = d_normed
         if side is yours:
             swap(15, s.d_normed.at[yours], s.d_normed_in)
+    early.across()
     swapped(15, s.d_normed_in)
     d_normed = s.d_normed[mine, :] + s.d_normed_in[...]
     unit = s.unit_zero[...]
-    s.few[0:1, :] = jnp.sum(d_normed * unit, 0, keepdims=True)
     d_first = s.d_second[...] + spread_back(unit, s.inverse_zero[:, :1], gain[0], d_normed)
     s.d_rows[mine, :] = d_first.astype(LOWF)
     swap(16, s.d_rows.at[mine], s.d_rows.at[mine])
+    s.few[0:1, :] = jnp.sum(d_normed * unit, 0, keepdims=True)
     s.few[4:5, :] = jnp.full((1, width), 0.5 * live.astype(WIDE), WIDE)
     swap(17, s.few, s.few_in)
     swapped(14, s.d_cand_in)
     for c in range(width // TILE):
         at = pl.ds(c * slots, slots)
         s.d_rows[slots:, c * TILE : (c + 1) * TILE] = (s.d_cand[at, :] + s.d_cand_in[at, :]).astype(LOWF)
+    over(
+        groups - 1,
+        lambda k: departed(
+            s.leaving.at[span((me + k + 1) % groups * half, half)], s.row_sent.at[(me + k + 1) % groups]
+        ),
+    )
+    early.settle()
+    swapped(16, s.d_rows.at[yours])
+
+    def give_rows(k):
+        tile = flipped(me // share, tiles - 1 - k)
+        number = s.flat[...] - (core * entries + tile * TILE)
+        hot = one_hot(tile_iota((TILE, entries), 0) == number)
+        picked = matmul(hot, s.d_rows[...]).astype(LOWF)
+        s.leaving[span(tile * TILE, TILE), :] = picked
+        into = s.arrived.at[core, span(me * half, half)]
+        for j in range(share):
+            owner = tile * share + j
+            block = s.leaving.at[span(owner * half, half)]
+
+            @pl.when(owner != me)
+            def _():
+                send(block, into, s.land_sent.at[owner], s.land_came.at[me], (owner, core))
+
+            @pl.when(owner == me)
+            def _():
+                s.arrived[core, span(me * half, half), :] = picked[j * half : (j + 1) * half]
+
+    over(tiles, give_rows)
     for c in range(3):
         late.source[c * width : (c + 1) * width, :] = matmul(s.normed_t[...], s.d_triple[c]).astype(LOWF)
     pos_at = 3 * width
     pos_half = places // 2
-    swapped(16, s.d_rows.at[yours])
     hot = one_hot(tile_iota((pos_half, slots), 0) + core * pos_half == s.place_row[...])
     late.source[pos_at : pos_at + pos_half, :] = matmul(hot, s.d_rows[:slots, :]).astype(LOWF)
     if pos_at + pos_half < late.source.shape[0]:
@@ -865,61 +902,30 @@
         send(s.few_all.at[me], s.few_all.at[me], s.few_sent.at[where], s.few_came.at[me], (where, core))
 
     over(groups - 1, give_few)
-    early.settle()
-
-    over(
-        groups - 1,
-        lambda k: departed(
-            s.leaving.at[span((me + k + 1) % groups * half, half)], s.row_sent.at[(me + k + 1) % groups]
-        ),
-    )
-
-    def give_rows(k):
-        tile = flipped(me // share, tiles - 1 - k)
-        number = s.flat[...] - (core * entries + tile * TILE)
-        hot = one_hot(tile_iota((TILE, entries), 0) == number)
-        picked = matmul(hot, s.d_rows[...]).astype(LOWF)
-        s.leaving[span(tile * TILE, TILE), :] = picked
-        into = s.landed.at[core, span(me * half, half)]
-        for j in range(share):
-            owner = tile * share + j
-            block = s.leaving.at[span(owner * half, half)]
-
-            @pl.when(owner != me)
-            def _():
-                send(block, into, s.land_sent.at[owner], s.land_came.at[me], (owner, core))
-
-            @pl.when(owner == me)
-            def _():
-                s.landed[core, span(me * half, half), :] = picked[j * half : (j + 1) * half]
-
-    over(tiles, give_rows)
+    early.forward()
     late.across()
-    early.forward()
-    late.settle()
     swapped(1, s.reqs.at[other])
     s.grad_table[...] = jnp.zeros(s.grad_table.shape, WIDE)
-    part = held // 7
 
     def gather(side, group):
-        came = s.landed[side, span(group * GROUP, GROUP), :]
+        came = s.arrived[side, span(group * GROUP, GROUP), :]
         first_row = core * held + 1
         lines = [s.reqs[side, pl.ds(2 * group + i, 1), :] - first_row for i in range(2)]
 
-        def block(b):
-            at = span(b * part, part, 8)
-            rows = tile_iota((part, TILE), 0) + b * part
-            hot = jnp.concatenate([one_hot(rows == line) for line in lines], 1)
-            s.grad_table[at, :] += matmul(hot, came)
-
-        over(7, block)
+        rows = tile_iota((held, TILE), 0)
+        hot = jnp.concatenate([one_hot(rows == line) for line in lines], 1)
+        s.grad_table[...] += matmul(hot, came)
 
     def between(k):
-        @pl.when(k == spans // 2)
+        @pl.when(k == 1)
+        def _():
+            late.settle()
+
+        @pl.when(k == 4)
         def _():
             late.forward()
 
-    take_all(s.landed, s.land_came, s.hand_sent, s.hand_came, gather, between)
+    take_all(s.arrived, s.land_came, s.hand_sent, s.hand_came, gather, between)
     final = s.grad_table[...]
     table_ref[...] = final
     square = (
@@ -966,6 +972,8 @@
     norm = jnp.sqrt(jnp.sum(s.squares[...], 0) + jnp.sum(gains * gains))
     stats_ref[...] = norm
 
+    for copy in keep:
+        copy.wait()
     early.drain()
     late.drain()
 
@@ -979,7 +987,6 @@
 
     def finish_group(group):
         block = s.arrived.at[core, span(group * GROUP, GROUP)]
-        departed(block, s.pass_sent.at[group])
         departed(block, s.hand_sent.at[group])
 
     over(spans, finish_group)
@@ -987,20 +994,27 @@
     ends = [s.table.at[rows_mine], s.reqs.at[core], s.w_out.at[core], s.w_up.at[core], s.w_down.at[core]]
     ends += [s.cands.at[mine], s.normed.at[mine]]
     ends += [s.mixed.at[hp, yours] for hp in range(2)] + [s.d_heads_out.at[hp] for hp in range(2)]
-    ends += [s.g_down.at[other], s.g_up.at[other], s.g_out.at[other], s.d_cand, s.d_normed.at[yours]]
+    ends += [s.g_down_out, s.g_up_out, s.g_out_out, s.d_cand, s.d_normed.at[yours]]
     ends += [s.d_rows.at[mine], s.few, position_own]
     for index, ref in enumerate(ends):
         departed(ref, s.sent.at[index])
 
 
-def run_step(table, attn_in, attn_out, ffn_up, ffn_down, position, owners, offsets, seg, live, logq, gains, groups):
+def in_hbm(array):
+    return pltpu.with_memory_space_constraint(array, pltpu.HBM)
+
+
+def run_step(trios, owners, offsets, seg, live, logq, gains, groups, keeps):
+    table, _, attn_out, ffn_up, _, position = (trio[0] for trio in trios)
     held, width = table.shape
     entries = owners.shape[1]
     heads_width, hidden, places = attn_out.shape[0], ffn_up.shape[1], position.shape[0]
     scratch = step_scratch(groups, held, entries, width, heads_width, hidden, places)
-    shape = jax.ShapeDtypeStruct
+    shape = pltpu.VMEM
+    arrays = [array for trio in trios for array in (trio if keeps else trio[:1])]
+    kept = arrays if keeps else []
     return pl.pallas_call(
-        functools.partial(step_kernel, groups, tuple(scratch)),
+        functools.partial(step_kernel, groups, keeps, tuple(scratch)),
         out_shape=(
             shape((held, width), WIDE),
             shape((heads_width + 2 * hidden, width), LOWF),
@@ -1008,14 +1022,15 @@
             shape((places, width), LOWF),
             shape((8, width), WIDE),
             shape((8, TILE), WIDE),
+            *(shape(array.shape, WIDE) for array in kept),
         ),
-        in_specs=[FAR] * 6 + [VMEM] * 3 + [SMEM] + [VMEM] * 2,
-        out_specs=(VMEM,) * 6,
+        in_specs=[VMEM] * 3 + [SMEM] + [VMEM] * 2 + [FAR] * len(arrays),
+        out_specs=(VMEM,) * (6 + len(kept)),
         scratch_shapes=list(scratch.values()),
         compiler_params=pltpu.CompilerParams(
-            collective_id=0, has_side_effects=True, vmem_limit_bytes=60 * 1024 * 1024
+            collective_id=0, has_side_effects=True, vmem_limit_bytes=(48 if keeps else 60) * 1024 * 1024
         ),
-    )(table, attn_in, attn_out, ffn_up, ffn_down, position, owners, offsets, seg, live, logq, gains)
+    )(owners, offsets, seg, live, logq, gains, *(in_hbm(array) for array in arrays))
 
 
 def adamw(weight, grad, first, second, decay, rate):
@@ -1025,11 +1040,13 @@
     return (weight - rate * (moved + decay * weight), first, second)
 
 
-def update_kernel(table_g, early_g, late_g, position_g, few_ref, stats_ref, *refs):
+def update_kernel(kept, table_g, early_g, late_g, position_g, few_ref, stats_ref, *refs):
     inputs, outputs, buffers = refs[:21], refs[21:45], refs[45:63]
     came, left = refs[63], refs[64]
     names = ("table", "in", "out", "up", "down", "position")
-    ins = [pltpu.make_async_copy(inputs[i], buffers[i], came.at[i]) for i in range(18)]
+    ins = []
+    if not kept:
+        ins = [pltpu.make_async_copy(inputs[i], buffers[i], came.at[i]) for i in range(18)]
     outs = [pltpu.make_async_copy(buffers[i], outputs[i], left.at[i]) for i in range(18)]
     for copy in ins:
         copy.start()
@@ -1047,16 +1064,21 @@
     block = 16
     for index, name in enumerate(names):
         trio = buffers[3 * index : 3 * index + 3]
-        for i in range(3):
-            ins[3 * index + i].wait()
+        sources = inputs[3 * index : 3 * index + 3] if kept else trio
+        for copy in ins[3 * index : 3 * index + 3]:
+            copy.wait()
         rate = RATE_POSITION if name == "position" else RATE
         lead = trio[0].shape[0] if name == "in" else 1
         rows, columns = trio[0].shape[-2:]
         heads_width, hidden = buffers[6].shape[0], buffers[9].shape[1]
 
-        def run(r, index=index, name=name, trio=trio, rows=rows, rate=rate):
+        def run(r, name=name, trio=trio, sources=sources, rows=rows, rate=rate):
             at = span(r * block, block)
-            views = [ref.at[r * block // rows, span(r * block % rows, block)] if name == "in" else ref.at[at] for ref in trio]
+
+            def view(ref):
+                return ref.at[r * block // rows, span(r * block % rows, block)] if name == "in" else ref.at[at]
+
+            values = [view(ref)[...] for ref in sources]
             if name == "table":
                 grad = table_g[at, :]
             elif name == "in":
@@ -1075,9 +1097,9 @@
                 grad = early_g[span(heads_width + hidden + r * block, block), :].astype(WIDE)
             else:
                 grad = position_g[at, :].astype(WIDE)
-            made = adamw(views[0][...], grad * factor, views[1][...], views[2][...], DECAY, rate)
-            for view, value in zip(views, made):
-                view[...] = value
+            made = adamw(values[0], grad * factor, values[1], values[2], DECAY, rate)
+            for ref, value in zip(trio, made):
+                view(ref)[...] = value
 
         over(lead * rows // block, run)
         for i in range(3):
@@ -1086,17 +1108,18 @@
         copy.wait()
 
 
-def run_update(grads, trios):
-    flat = [array for trio in trios for array in trio]
+def run_update(grads, trios, kept):
+    flat = [*kept] if kept else [in_hbm(array) for trio in trios[:6] for array in trio]
+    flat += trios[6]
     shape = jax.ShapeDtypeStruct
     scalar = shape((1, 1), WIDE)
     return pl.pallas_call(
-        update_kernel,
+        functools.partial(update_kernel, bool(kept)),
         out_shape=tuple(shape(a.shape, WIDE) for a in flat) + (scalar,) * 3,
-        in_specs=[VMEM] * 5 + [VMEM] + [FAR] * 18 + [VMEM] * 3,
+        in_specs=[VMEM] * 6 + [VMEM if kept else FAR] * 18 + [VMEM] * 3,
         out_specs=(FAR,) * 18 + (VMEM,) * 3 + (SMEM,) * 3,
         scratch_shapes=[pltpu.VMEM(a.shape, WIDE) for a in flat[:18]] + [DMA((18,)), DMA((18,))],
-        compiler_params=pltpu.CompilerParams(vmem_limit_bytes=60 * 1024 * 1024),
+        compiler_params=pltpu.CompilerParams(vmem_limit_bytes=(24 if kept else 48) * 1024 * 1024),
     )(*grads, *flat)
 
 
@@ -1128,33 +1151,28 @@
     live_slots,
     log_freq,
 ):
+    trios = (
+        (item_table, item_first, item_second),
+        (attn_in, attn_in_first, attn_in_second),
+        (attn_out, attn_out_first, attn_out_second),
+        (ffn_up, ffn_up_first, ffn_up_second),
+        (ffn_down, ffn_down_first, ffn_down_second),
+        (position_table, position_first, position_second),
+        (norm_gains, gains_first, gains_second),
+    )
+    groups = lax.axis_size("dp")
     grads = run_step(
-        item_table,
-        attn_in,
-        attn_out,
-        ffn_up,
-        ffn_down,
-        position_table,
+        trios[:6],
         owner_group.reshape(1, -1),
         row_offset,
         segment_ids,
         live_slots,
         log_freq,
         norm_gains,
-        lax.axis_size("dp"),
+        groups,
+        groups <= 16,
     )
-    made = run_update(
-        grads,
-        (
-            (item_table, item_first, item_second),
-            (attn_in, attn_in_first, attn_in_second),
-            (attn_out, attn_out_first, attn_out_second),
-            (ffn_up, ffn_up_first, ffn_up_second),
-            (ffn_down, ffn_down_first, ffn_down_second),
-            (position_table, position_first, position_second),
-            (norm_gains, gains_first, gains_second),
-        ),
-    )
+    made = run_update(grads[:6], trios, grads[6:])
     return (*made[:21], *(scalar.reshape(()) for scalar in made[21:]))
 
 

time: 157 us -> 136 us (0.87)
  Pallas kernels: 155 us -> 134 us
    pallas_call x2, Pallas kernels: 155 us -> 134 us  [the longest x1 126 us: run_step(): pl.pallas_call(functools.partial(step_kernel, groups, keeps, tuple(scratc...]
where the time goes in v2:
time: 136 us
  Pallas kernels  134 us (99%)
  between operations  1.51 us (1%)
    pallas_call x1, Pallas kernels, run_step(): pl.pallas_call(functools.partial(step_kernel, groups, keeps, tuple(scratc...  126 us
    pallas_call x1, Pallas kernels, run_update(): pl.pallas_call(functools.partial(update_kernel, bool(kept)), out_shape=tu...  8.04 us

profile of v2, /device:TPU:0, one launch (start us, length us, event | category | flops | bytes accessed | tf_op | source)
XLA Modules:
  0.0 135.9 jit_solution(13784781642841395266)
XLA Ops:
  1.3 125.6 %shard_map.433 = (f32[784,256]{1,0:T(8,128)S(1)}, bf16[1280,256]{1,0:T(8,128)(2,1)S(1)}, bf16[768,256]{1,0:T(8,128)(2,1)S(1)}, bf16[512,256]{1,0:T(8,128)(2,1)S(...) custom-call(s32[1,2048]{1,0:T(1,128)} %bitcast.4, ...), custom_call_target="tpu_custom_call" | custom-call | tf_op jit(solution)/shard_map/pallas_call | solution.py:1016
  127.0 0.0 copy-start.2
  127.0 0.0 copy-start.1
  127.0 0.0 copy-start
  127.0 0.7 copy-done.2
  127.7 0.0 copy-done.1
  127.7 0.0 copy-done
  127.7 8.0 %shard_map.434 = (f32[784,256]{1,0:T(8,128)}, f32[784,256]{1,0:T(8,128)}, f32[784,256]{1,0:T(8,128)}, f32[3,256,256]{2,1,0:T(8,128)}, f32[3,256,256]{2,1,0:T(8,1...) custom-call(f32[784,256]{1,0:T(8,128)S(1)} %get-tuple-element.72.tab, ...), custom_call_target="tpu_custom_call" | custom-call | tf_op jit(solution)/shard_map/pallas_call | solution.py:1116
Async XLA Ops:
  127.0 0.7 copy-start.2
  127.0 0.7 copy-start.1
  127.0 0.7 copy-start

commit v3 on v2

--- a/solution.py
+++ b/solution.py
@@ -134,25 +134,28 @@
         name + "_half": pltpu.VMEM((outer * shard, width), LOWF),
         name + "_column": pltpu.VMEM((outer, shard, width), LOWF),
         name + "_shard": pltpu.VMEM((shard, width), WIDE),
+        name + "_whole": pltpu.VMEM((groups * shard, width), LOWF),
         name + "_plane_sent": DMA((inner,)),
         name + "_plane_came": DMA((inner,)),
         name + "_column_sent": DMA((outer,)),
         name + "_column_came": DMA((outer,)),
         name + "_out_sent": DMA((outer,)),
-        name + "_ahead_sent": DMA((groups,)),
-        name + "_came": DMA((groups,)),
+        name + "_ahead_sent": DMA((inner,)),
+        name + "_ahead_came": DMA((inner,)),
+        name + "_came": DMA((outer,)),
     }
 
 
 class Part:
-    def __init__(self, scratch, name, whole, groups, me, core):
+    def __init__(self, scratch, name, groups, me, core):
         for key, ref in vars(scratch).items():
             if key.startswith(name + "_"):
                 setattr(self, key[len(name) + 1 :], ref)
-        self.whole, self.me, self.core = whole, me, core
+        self.me, self.core = me, core
         self.inner, self.outer = levels_of(groups)
         self.i, self.o = me % self.inner, me // self.inner
         self.size = self.shard.shape[0]
+        self.rounds = self.outer.bit_length() - 1
 
     def quarter(self, j):
         return span(j * self.outer * self.size, self.outer * self.size)
@@ -169,28 +172,49 @@
             (self.o * self.inner + j, self.core),
         )
 
-    def column_copy(self, o):
+    def mate(self, bit):
+        return self.o + (1 - 2 * (self.o // 2**bit % 2)) * 2**bit
+
+    def column_copy(self, bit, index):
+        mate = self.mate(bit)
+        low = mate % 2 ** (bit + 1)
+        source = low + index * 2 ** (bit + 1)
+        slot = self.outer - self.outer // 2**bit + index
         return copy_to(
-            self.half.at[span(o * self.size, self.size)],
-            self.column.at[self.o],
-            self.column_sent.at[o],
-            self.column_came.at[self.o],
-            (o * self.inner + self.i, self.core),
+            self.half.at[span(source * self.size, self.size)],
+            self.column.at[slot],
+            self.column_sent.at[slot],
+            self.column_came.at[slot],
+            (mate * self.inner + self.i, self.core),
         )
 
-    def out_copy(self, o):
-        block = self.whole.at[self.piece(self.i, self.o)]
-        came = self.came.at[self.i * self.outer + self.o]
-        return copy_to(block, block, self.out_sent.at[o], came, (o * self.inner + self.i, self.core))
-
-    def ahead_copy(self, o, j):
+    def out_copy(self, bit, index):
+        o = self.o % 2 ** (bit + 1) + index * 2 ** (bit + 1)
         block = self.whole.at[self.piece(self.i, o)]
-        came = self.came.at[self.i * self.outer + o]
-        sent = self.ahead_sent.at[j * self.outer + o]
+        return copy_to(
+            block,
+            block,
+            self.out_sent.at[self.outer - self.outer // 2**bit + index],
+            self.came.at[o],
+            (self.mate(bit) * self.inner + self.i, self.core),
+        )
+
+    def ahead_copy(self, j):
+        block = self.whole.at[self.quarter(self.i)]
+        sent, came = self.ahead_sent.at[j], self.ahead_came.at[self.i]
         return copy_to(block, block, sent, came, (self.o * self.inner + j, self.core))
 
     def wait(self, ref, semaphore):
         copy_to(ref, ref, semaphore, semaphore, (self.me, self.core)).wait_recv()
+
+    def fill(self, blocks, at=0):
+        for block in blocks:
+            self.source[at : at + block.shape[0], :] = block.astype(LOWF)
+            at += block.shape[0]
+        if at < self.source.shape[0]:
+            shape = (self.source.shape[0] - at, self.source.shape[1])
+            self.source[at:, :] = jnp.zeros(shape, LOWF)
+        self.start()
 
     def start(self):
         over(self.inner - 1, lambda k: self.plane_copy((self.i + k + 1) % self.inner).start())
@@ -202,57 +226,74 @@
             self.wait(self.plane.at[j], self.plane_came.at[j])
             total = total + self.plane[j].astype(WIDE)
         self.half[...] = total.astype(LOWF)
-        over(self.outer - 1, lambda k: self.column_copy((self.o + k + 1) % self.outer).start())
-
-    def settle(self):
-        self.shard[...] = self.half[span(self.o * self.size, self.size), :].astype(WIDE)
-
-        def take(k):
-            o = (self.o + k + 1) % self.outer
-            self.wait(self.column.at[o], self.column_came.at[o])
-            self.shard[...] += self.column[o].astype(WIDE)
-
-        over(self.outer - 1, take)
-        self.whole[self.piece(self.i, self.o), :] = self.shard[...].astype(LOWF)
-        over(self.outer - 1, lambda k: self.out_copy((self.o + k + 1) % self.outer).start())
-        self.pass_on(self.o)
-
-    def pass_on(self, o):
-        over(self.inner - 1, lambda k: self.ahead_copy(o, (self.i + k + 1) % self.inner).start())
-
-    def forward(self):
-        def step(k):
-            o = (self.o + k + 1) % self.outer
-            block = self.whole.at[self.piece(self.i, o)]
-            self.wait(block, self.came.at[self.i * self.outer + o])
-            self.pass_on(o)
-
-        over(self.outer - 1, step)
+        self.halve(0)
+
+    def halve(self, bit):
+        over(self.outer // 2 ** (bit + 1), lambda k: self.column_copy(bit, k).start())
+
+    def settle(self, bits):
+        for bit in bits:
+            count = self.outer // 2 ** (bit + 1)
+
+            def take(k, bit=bit):
+                slot = self.outer - self.outer // 2**bit + k
+                self.wait(self.column.at[slot], self.column_came.at[slot])
+                o = self.o % 2 ** (bit + 1) + k * 2 ** (bit + 1)
+                at = span(o * self.size, self.size)
+                total = self.half[at, :].astype(WIDE) + self.column[slot].astype(WIDE)
+                self.half[at, :] = total.astype(LOWF)
+                if bit == self.rounds - 1:
+                    self.shard[...] = total
+                    self.whole[self.piece(self.i, self.o), :] = total.astype(LOWF)
+
+            over(count, take)
+            if bit < self.rounds - 1:
+                self.halve(bit + 1)
+            else:
+                self.double(bit)
+
+    def double(self, bit):
+        over(self.outer // 2 ** (bit + 1), lambda k: self.out_copy(bit, k).start())
+
+    def forward(self, bits):
+        for bit in bits:
+
+            def step(k, bit=bit):
+                o = self.mate(bit) % 2 ** (bit + 1) + k * 2 ** (bit + 1)
+                self.wait(self.whole.at[self.piece(self.i, o)], self.came.at[o])
+
+            over(self.outer // 2 ** (bit + 1), step)
+            if bit > 0:
+                self.double(bit - 1)
+            else:
+                over(self.inner - 1, lambda k: self.ahead_copy((self.i + k + 1) % self.inner).start())
 
     def collect(self):
         def step(k):
-            j = (self.i + k // self.outer + 1) % self.inner
-            o = k % self.outer
-            block = self.whole.at[self.piece(j, o)]
-            self.wait(block, self.came.at[j * self.outer + o])
-
-        over((self.inner - 1) * self.outer, step)
+            j = (self.i + k + 1) % self.inner
+            self.wait(self.whole.at[self.quarter(j)], self.ahead_came.at[j])
+
+        over(self.inner - 1, step)
 
     def drain(self):
         over(self.inner - 1, lambda k: self.plane_copy((self.i + k + 1) % self.inner).wait_send())
 
-        def far(k):
-            o = (self.o + k + 1) % self.outer
-            self.column_copy(o).wait_send()
-            self.out_copy(o).wait_send()
-
-        over(self.outer - 1, far)
-
-        def near(k):
-            j = (self.i + k // self.outer + 1) % self.inner
-            self.ahead_copy(k % self.outer, j).wait_send()
-
-        over((self.inner - 1) * self.outer, near)
+        for bit in range(self.rounds):
+
+            def far(k, bit=bit):
+                self.column_copy(bit, k).wait_send()
+                self.out_copy(bit, k).wait_send()
+
+            over(self.outer // 2 ** (bit + 1), far)
+
+        over(self.inner - 1, lambda k: self.ahead_copy((self.i + k + 1) % self.inner).wait_send())
+
+
+def part_rows(width, heads_width, hidden, places):
+    return {
+        "early": heads_width + 2 * hidden,
+        "late": 3 * width + places // 2,
+    }
 
 
 def step_scratch(groups, held, entries, width, heads_width, hidden, places):
@@ -262,14 +303,16 @@
     area = windows(slots)[1]
     blocks = slots // TILE
     padded = -(-2 * held // TILE) * TILE
+    bank = entries // TILE // 2
     shapes = {
         "table": ((padded, width), LOWF),
         "flat": ((1, entries), jnp.int32),
         "want": ((groups, 8, TILE), jnp.int32),
         "asked": ((groups, 8, TILE), jnp.int32),
         "reqs": ((2, entries // TILE, TILE), jnp.int32),
-        "leaving": ((entries, width), LOWF),
-        "arrived": ((2, entries, width), LOWF),
+        "leaving": ((2, bank, TILE, width), LOWF),
+        "arrived": ((2, 2, bank, TILE, width), LOWF),
+        "landed": ((2, 2, bank, TILE, width), LOWF),
         "cands": ((slots, width), LOWF),
         "w_out": ((2, heads_width, width), LOWF),
         "w_up": ((2, width, hidden), LOWF),
@@ -288,6 +331,7 @@
         "keys_t": ((pairs, TILE, slots), LOWF),
         "values_t": ((pairs, TILE, slots), LOWF),
         "probs": ((pairs, area, 2 * TILE), WIDE),
+        "scales": ((pairs, max(8, blocks), 2 * TILE), WIDE),
         "mixed": ((pairs, slots, TILE), LOWF),
         "mixed_in": ((pairs, own, TILE), LOWF),
         "joined": ((2, own, heads_width), LOWF),
@@ -327,9 +371,6 @@
         "few": ((8, width), WIDE),
         "few_in": ((8, width), WIDE),
         "few_all": ((groups, 8, width), WIDE),
-        "squares": ((2 * groups, 8, TILE), WIDE),
-        "early_whole": ((groups * shard_rows(2 * hidden + heads_width, groups), width), LOWF),
-        "late_whole": ((groups * shard_rows(3 * heads_width + places // 2, groups), width), LOWF),
         "other_half": ((places // 2, width), LOWF),
     }
     scratch = {name: pltpu.VMEM(*entry) for name, entry in shapes.items()}
@@ -337,15 +378,13 @@
         scratch[name + "_sent"] = DMA((groups,))
         scratch[name + "_came"] = DMA((groups,))
     for name in ("pass", "hand"):
-        scratch[name + "_sent"] = DMA((entries // GROUP,))
-        scratch[name + "_came"] = DMA((entries // GROUP,))
-    scratch["square_sent"] = DMA((2 * groups,))
-    scratch["square_came"] = DMA((2 * groups,))
+        scratch[name + "_sent"] = DMA((bank,))
+        scratch[name + "_came"] = DMA((bank,))
     scratch["sent"] = DMA((LINKS,))
     scratch["came"] = DMA((LINKS,))
     scratch["loads"] = DMA((24,))
-    scratch.update(part_scratch("early", 2 * hidden + heads_width, width, groups))
-    scratch.update(part_scratch("late", 3 * heads_width + places // 2, width, groups))
+    for name, rows in part_rows(width, heads_width, hidden, places).items():
+        scratch.update(part_scratch(name, rows, width, groups))
     return scratch
 
 
@@ -354,8 +393,8 @@
     count = 18 if keeps else 6
     fars, refs = refs[6 : 6 + count], refs[6 + count :]
     table_far, in_far, out_far, up_far, down_far, pos_far = fars[:: count // 6]
-    (table_ref, early_ref, late_ref, position_ref, few_ref, stats_ref) = refs[:6]
-    nears, refs = (refs[6:24], refs[24:]) if keeps else (None, refs[6:])
+    (table_ref, down_ref, mid_ref, inward_ref, position_ref, few_ref, stats_ref) = refs[:7]
+    nears, refs = (refs[7:25], refs[25:]) if keeps else (None, refs[7:])
     s = types.SimpleNamespace(**dict(zip(names, refs)))
     me, core = lax.axis_index("dp"), lax.axis_index("ffn")
     other = 1 - core
@@ -370,8 +409,7 @@
     pairs, hidden, places = s.keys.shape[0], s.w_up.shape[2], pos_far.shape[0]
     heads_width = pairs * TILE
     mine, yours = span(core * own, own), span(other * own, own)
-    early = Part(s, "early", s.early_whole, groups, me, core)
-    late = Part(s, "late", s.late_whole, groups, me, core)
+    early, late = sums = [Part(s, name, groups, me, core) for name in ("early", "late")]
 
     barrier = pltpu.get_barrier_semaphore()
     slot_of = me * 2 + core
@@ -482,8 +520,27 @@
     swapped(0, s.table.at[rows_yours])
     lanes_wide = tile_iota((TILE, TILE), 1).astype(WIDE)
 
-    def serve(k):
-        tile = flipped(me // share, tiles - 1 - k)
+    bank = tiles // 2
+
+    def seat(number):
+        tile = number // share
+        return tile // bank, tile % bank, span(number % share * half, half)
+
+    def ship(tile, picked, buffer, sent, came):
+        s.leaving[tile // bank, tile % bank] = picked
+        for j in range(share):
+            number = tile * share + j
+
+            @pl.when(number != me)
+            def _():
+                block = s.leaving.at[seat(number)]
+                send(block, buffer.at[(core, *seat(me))], sent.at[number], came.at[me], (number, core))
+
+            @pl.when(number == me)
+            def _():
+                buffer[(core, *seat(me))] = picked[j * half : (j + 1) * half]
+
+    def serve(tile):
         line = jnp.zeros((1, TILE), jnp.int32)
         for j in range(share):
             source = tile * share + j
@@ -504,115 +561,109 @@
             1,
         )
         picked = matmul(hot, s.table[...]).astype(LOWF)
-        s.leaving[span(tile * TILE, TILE), :] = picked
-        into = s.arrived.at[core, span(me * half, half)]
-        for j in range(share):
-            source = tile * share + j
-            block = s.leaving.at[span(source * half, half)]
-
-            @pl.when(source != me)
-            def _():
-                send(block, into, s.row_sent.at[source], s.row_came.at[me], (source, core))
-
-            @pl.when(source == me)
-            def _():
-                s.arrived[core, span(me * half, half), :] = picked[j * half : (j + 1) * half]
-
-    over(tiles, serve)
-    swap(1, s.reqs.at[core], s.reqs.at[core])
-
-    for load in loads[1:]:
-        load.wait()
+        ship(tile, picked, s.arrived, s.row_sent, s.row_came)
+
     keep = []
     if keeps:
         for i in range(12):
             index = i // 2 * 3 + 1 + i % 2
             keep.append(pltpu.make_async_copy(fars[index], nears[index], s.loads.at[12 + i]))
-            keep[-1].start()
-    s.w_out[core] = staged[1][...].astype(LOWF)
-    swap(2, s.w_out.at[core], s.w_out.at[core])
-    ups = hidden // width
-    for c in range(ups):
-        s.w_up[core, :, c * width : (c + 1) * width] = staged[2 + c][...].astype(LOWF)
-    swap(3, s.w_up.at[core], s.w_up.at[core])
-    s.w_down[core] = staged[2 + ups][...].astype(LOWF)
-    swap(4, s.w_down.at[core], s.w_down.at[core])
-    for c in range(3):
-        s.w_in[c] = staged[3 + ups + c][...].astype(LOWF)
-    high = staged[-1][...].astype(LOWF)
-    s.pos_high[...] = high
-    s.pos_low[...] = (staged[-1][...] - high.astype(WIDE)).astype(LOWF)
-    seg = seg_ref[...]
-    level = tile_iota((LEVELS, slots), 0)
-    starts = jnp.sum(jnp.where(seg < level, 1.0, 0.0), 1, keepdims=True)
-    start = jnp.sum(jnp.where(seg == level, starts, 0.0), 0, keepdims=True)
-    place_row = tile_iota((1, slots), 1) - start.astype(jnp.int32)
-    s.place_row[...] = place_row
-    seg_wide = seg.astype(WIDE)
-    for b in range(slots // TILE):
-        at = slice(b * TILE, (b + 1) * TILE)
-        s.segments[at, :] = as_column(seg_wide[:, at], eye, ones)
-        s.place[at, :] = column_of(place_row[:, at])
     found, _ = windows(slots)
-    causal = tile_iota((TILE, TILE), 0) <= tile_iota((TILE, TILE), 1)
-    for b, low, wide, at in found:
-        line = seg_wide[:, b * TILE : (b + 1) * TILE]
-        for t in range(wide // TILE):
-            same = s.segments[low + t * TILE : low + (t + 1) * TILE, :] == line
-            if low + t * TILE == b * TILE:
-                same = same & causal
-            s.bias[at + t * TILE : at + (t + 1) * TILE, :] = jnp.where(same, 0.0, LOWEST)
     live = live_ref[0]
-    alive_row = tile_iota((1, slots), 1) < live
-    s.logit_bias[...] = jnp.where(alive_row, -logq_ref[...], LOWEST)
     first_lanes = (tile_iota((1, TILE), 1) < HEAD).astype(WIDE)
     pick = [first_lanes.astype(LOWF), (1.0 - first_lanes).astype(LOWF)]
     gain = [gain_ref[g : g + 1, :] for g in range(3)]
     step = 2 * TILE
 
-    def group_at(k):
-        near = spans // 2
-        turn = jnp.where(k < near // 2, k, jnp.where(k < near // 2 + near, k + near // 2, k - near))
-        return flipped(me * half // GROUP, spans - 1 - turn, 3)
-
-    def lay(side, group):
-        came = s.arrived[side, span(group * GROUP, GROUP), :]
-        where = s.column[...] - (side * entries + group * GROUP).astype(WIDE)
+
+    def prepare():
+        for load in loads[1:]:
+            load.wait()
+        for copy in keep:
+            copy.start()
+        s.w_out[core] = staged[1][...].astype(LOWF)
+        ups = hidden // width
+        for c in range(ups):
+            s.w_up[core, :, c * width : (c + 1) * width] = staged[2 + c][...].astype(LOWF)
+        s.w_down[core] = staged[2 + ups][...].astype(LOWF)
+        for c in range(3):
+            s.w_in[c] = staged[3 + ups + c][...].astype(LOWF)
+        high = staged[-1][...].astype(LOWF)
+        s.pos_high[...] = high
+        s.pos_low[...] = (staged[-1][...] - high.astype(WIDE)).astype(LOWF)
+        seg = seg_ref[...]
+        level = tile_iota((LEVELS, slots), 0)
+        starts = jnp.sum(jnp.where(seg < level, 1.0, 0.0), 1, keepdims=True)
+        start = jnp.sum(jnp.where(seg == level, starts, 0.0), 0, keepdims=True)
+        place_row = tile_iota((1, slots), 1) - start.astype(jnp.int32)
+        s.place_row[...] = place_row
+        seg_wide = seg.astype(WIDE)
+        for b in range(slots // TILE):
+            at = slice(b * TILE, (b + 1) * TILE)
+            s.segments[at, :] = as_column(seg_wide[:, at], eye, ones)
+            s.place[at, :] = column_of(place_row[:, at])
+        causal = tile_iota((TILE, TILE), 0) <= tile_iota((TILE, TILE), 1)
+        for b, low, wide, at in found:
+            line = seg_wide[:, b * TILE : (b + 1) * TILE]
+            for t in range(wide // TILE):
+                same = s.segments[low + t * TILE : low + (t + 1) * TILE, :] == line
+                if low + t * TILE == b * TILE:
+                    same = same & causal
+                s.bias[at + t * TILE : at + (t + 1) * TILE, :] = jnp.where(same, 0.0, LOWEST)
+        alive_row = tile_iota((1, slots), 1) < live
+        s.logit_bias[...] = jnp.where(alive_row, -logq_ref[...], LOWEST)
+        for index, block in enumerate((s.w_out, s.w_up, s.w_down)):
+            swap(2 + index, block.at[core], block.at[core])
+
+    def spot_of(h):
+        return flipped(me // share % bank, bank - 1 - h)
+
+    def pair_of(buffer, side, spot):
+        return jnp.concatenate([buffer[side, 0, spot], buffer[side, 1, spot]], 0)
+
+    def lay(side, spot):
         lane = tile_iota((slots, TILE), 1).astype(WIDE)
-        hot = jnp.concatenate([one_hot(where == lane), one_hot(where == lane + float(TILE))], 1)
-        s.total[...] += matmul(hot, came)
-
-    def take(k, buffer, came, sent_on, passed, use):
-        group = group_at(k)
-        for j in range(GROUP // half):
-            owner = group * (GROUP // half) + j
-
-            @pl.when(owner != me)
+        firsts = [(side * entries + (spot + b * bank) * TILE).astype(WIDE) for b in range(2)]
+        hot = jnp.concatenate([one_hot(s.column[...] - first == lane) for first in firsts], 1)
+        s.total[...] += matmul(hot, pair_of(s.arrived, side, spot))
+
+    def trade(ahead, give, buffer, came, sent_on, passed, use, between):
+        def other_two(h):
+            spot = spot_of(h)
+            arrived(buffer.at[other, :, spot], passed.at[spot])
+            use(other, spot)
+
+        def receive(h):
+            spot = spot_of(h)
+            for b in range(2):
+                for j in range(share):
+                    number = (spot + b * bank) * share + j
+
+                    @pl.when(number != me)
+                    def _():
+                        arrived(buffer.at[(core, *seat(number))], came.at[number])
+
+            block = buffer.at[core, :, spot]
+            send(block, block, sent_on.at[spot], passed.at[spot], (me, other))
+            use(core, spot)
+            pl.when(h > 0)(lambda: other_two(h - 1))
+
+        def step(h):
+            @pl.when(h < bank)
             def _():
-                arrived(buffer.at[core, span(owner * half, half)], came.at[owner])
-
-        block = buffer.at[core, span(group * GROUP, GROUP)]
-        send(block, block, sent_on.at[group], passed.at[group], (me, other))
-        use(core, group)
-
-        @pl.when(k > 0)
-        def _():
-            last = group_at(k - 1)
-            arrived(buffer.at[other, span(last * GROUP, GROUP)], passed.at[last])
-            use(other, last)
-
-    def take_all(buffer, came, sent_on, passed, use, between=None):
-        def run(k):
-            take(k, buffer, came, sent_on, passed, use)
-            if between is not None:
-                between(k)
-
-        over(spans, run)
-        last = group_at(jnp.int32(spans - 1))
-        arrived(buffer.at[other, span(last * GROUP, GROUP)], passed.at[last])
-        use(other, last)
-
-    take_all(s.arrived, s.row_came, s.pass_sent, s.pass_came, lay)
+                spot = spot_of(h)
+                far = 1 - me // share // bank
+                give(spot + far * bank)
+                give(spot + (1 - far) * bank)
+
+            between(h)
+            pl.when(h >= ahead)(lambda: receive(h - ahead))
+
+        over(bank + ahead, step)
+        other_two(jnp.int32(bank - 1))
+
+    trade(3, serve, s.arrived, s.row_came, s.pass_sent, s.pass_came, lay, lambda h: pl.when(h == 2)(prepare))
+    swap(1, s.reqs.at[core], s.reqs.at[core])
     s.cands[mine, :] = s.total[own:, :].astype(LOWF)
     swap(5, s.cands.at[mine], s.cands.at[mine])
 
@@ -669,9 +720,10 @@
             bias = s.bias[at : at + wide, :]
             scores = scores + jnp.concatenate([bias, bias], 1)
             expo = jnp.exp(scores - jnp.max(scores, 0, keepdims=True))
-            prob = expo * (1.0 / jnp.sum(expo, 0, keepdims=True))
-            s.probs[hp, at : at + wide, :] = prob
-            out = matmul(s.values_t[hp, :, low : low + wide], prob.astype(LOWF))
+            scale = 1.0 / jnp.sum(expo, 0, keepdims=True)
+            s.scales[hp, b : b + 1, :] = scale
+            s.probs[hp, at : at + wide, :] = expo
+            out = matmul(s.values_t[hp, :, low : low + wide], expo.astype(LOWF)) * scale
             out = jnp.concatenate([out[:HEAD, :TILE], out[HEAD:, TILE:]], 0)
             s.mixed[hp, b * TILE : (b + 1) * TILE, :] = out.T.astype(LOWF)
         swap(7 + hp, s.mixed.at[hp, yours], s.mixed_in.at[hp])
@@ -679,7 +731,7 @@
     over(pairs, attend)
     for index, block in enumerate((s.w_out, s.w_up, s.w_down)):
         swapped(2 + index, block.at[other])
-    over(spans, lambda g: departed(s.arrived.at[core, span(g * GROUP, GROUP)], s.pass_sent.at[g]))
+    over(bank, lambda spot: departed(s.arrived.at[core, :, spot], s.pass_sent.at[spot]))
     for hp in range(pairs):
         swapped(7 + hp, s.mixed_in.at[hp])
 
@@ -726,19 +778,25 @@
 
     def choose(r):
         at = span(r * TILE, TILE)
-        logits = matmul(s.final[at, :], s.cands[...], NT) + s.logit_bias[...]
-        number = tile_iota((TILE, slots), 0) + (core * own + r * TILE)
-        same = tile_iota((TILE, slots), 1) == number
+        here = span(core * own + r * TILE, TILE, TILE)
+        final = s.final[at, :]
+        logits = matmul(final, s.cands[...], NT) + s.logit_bias[...]
+        square = matmul(final, s.cands[here, :], NT) + s.logit_bias[:, here]
+        same = tile_iota((TILE, TILE), 0) == tile_iota((TILE, TILE), 1)
+        number = tile_iota((TILE, 1), 0) + (core * own + r * TILE)
         top = jnp.max(logits, -1, keepdims=True)
         expo = jnp.exp(logits - top)
         total = jnp.sum(expo, -1, keepdims=True)
-        alive = number[:, :1] < live
-        right = jnp.sum(jnp.where(same, logits, 0.0), -1, keepdims=True)
+        alive = number < live
+        right = jnp.sum(jnp.where(same, square, 0.0), -1, keepdims=True)
         loss = jnp.sum(jnp.where(alive, top + jnp.log(total) - right, 0.0))
         s.few[3:4, :] += jnp.full((1, width), loss, WIDE)
         alive = jnp.where(alive, 1.0, 0.0)
-        grad = (expo * (alive / total) - jnp.where(same, alive, 0.0)).astype(LOWF)
-        s.d_logits[at, :] = grad
+        scale = alive / total
+        s.d_logits[at, :] = (expo * scale).astype(LOWF)
+        square = jnp.exp(square - top) * scale - jnp.where(same, alive, 0.0)
+        s.d_logits[at, here] = square.astype(LOWF)
+        grad = s.d_logits[at, :]
         d_final = matmul(grad, s.cands[...])
         unit = s.unit_two[at, :]
         s.few[2:3, :] += jnp.sum(d_final * unit, 0, keepdims=True)
@@ -790,23 +848,20 @@
     s.d_keys[...] = jnp.zeros(s.d_keys.shape, WIDE)
     s.d_values[...] = jnp.zeros(s.d_values.shape, WIDE)
 
-    def give_early():
+    def give_mid():
         swapped(11, s.g_down_in)
         swapped(12, s.g_up_in)
         swapped(13, s.g_out_in)
         g_up = s.g_up[...] + s.g_up_in[...].astype(WIDE)
-        at = 0
-        for block in (
-            s.g_out[...] + s.g_out_in[...].astype(WIDE),
-            *(g_up[:, c * width : (c + 1) * width] for c in range(hidden // width)),
-            s.g_down[...] + s.g_down_in[...].astype(WIDE),
-        ):
-            early.source[at : at + block.shape[0], :] = block.astype(LOWF)
-            at += block.shape[0]
-        if at < early.source.shape[0]:
-            early.source[at:, :] = jnp.zeros((early.source.shape[0] - at, width), LOWF)
-        early.start()
-
+        early.fill(
+            (
+                s.g_out[...] + s.g_out_in[...].astype(WIDE),
+                *(g_up[:, c * width : (c + 1) * width] for c in range(hidden // width)),
+                s.g_down[...] + s.g_down_in[...].astype(WIDE),
+            )
+        )
+
+    give_mid()
     for hp in range(pairs):
         swapped(9 + hp, s.d_heads.at[hp, yours])
 
@@ -815,7 +870,7 @@
             d_block = s.d_heads[hp, b * TILE : (b + 1) * TILE, :]
             d_pair = jnp.concatenate([d_block * pick[0], d_block * pick[1]], 0)
             d_prob = matmul(s.values[hp, low : low + wide, :], d_pair, NT)
-            prob = s.probs[hp, at : at + wide, :]
+            prob = s.probs[hp, at : at + wide, :] * s.scales[hp, b : b + 1, :]
             mean = jnp.sum(prob * d_prob, 0, keepdims=True)
             d_scores = (prob * (d_prob - mean)).astype(LOWF)
             s.d_keys[hp, low : low + wide, :] += matmul(d_scores, s.queries[hp, b])
@@ -824,8 +879,6 @@
             out = jnp.concatenate([out[:HEAD, :TILE], out[HEAD:, TILE:]], 0) * SCALE
             lanes = span(hp * TILE, TILE, TILE)
             s.d_triple[0, b * TILE : (b + 1) * TILE, lanes] = out.T.astype(LOWF)
-            if b == 3:
-                pl.when(hp == 0)(give_early)
 
 
     over(pairs, attend_back)
@@ -840,6 +893,9 @@
         s.d_normed[side, :] = d_normed
         if side is yours:
             swap(15, s.d_normed.at[yours], s.d_normed_in)
+    for c in range(3):
+        g_in = matmul(s.normed_t[...], s.d_triple[c])
+        late.source[c * width : (c + 1) * width, :] = g_in.astype(LOWF)
     early.across()
     swapped(15, s.d_normed_in)
     d_normed = s.d_normed[mine, :] + s.d_normed_in[...]
@@ -849,7 +905,6 @@
     swap(16, s.d_rows.at[mine], s.d_rows.at[mine])
     s.few[0:1, :] = jnp.sum(d_normed * unit, 0, keepdims=True)
     s.few[4:5, :] = jnp.full((1, width), 0.5 * live.astype(WIDE), WIDE)
-    swap(17, s.few, s.few_in)
     swapped(14, s.d_cand_in)
     for c in range(width // TILE):
         at = pl.ds(c * slots, slots)
@@ -857,98 +912,78 @@
     over(
         groups - 1,
         lambda k: departed(
-            s.leaving.at[span((me + k + 1) % groups * half, half)], s.row_sent.at[(me + k + 1) % groups]
+            s.leaving.at[seat((me + k + 1) % groups)], s.row_sent.at[(me + k + 1) % groups]
         ),
     )
-    early.settle()
     swapped(16, s.d_rows.at[yours])
 
-    def give_rows(k):
-        tile = flipped(me // share, tiles - 1 - k)
+    def give_rows(tile):
         number = s.flat[...] - (core * entries + tile * TILE)
         hot = one_hot(tile_iota((TILE, entries), 0) == number)
         picked = matmul(hot, s.d_rows[...]).astype(LOWF)
-        s.leaving[span(tile * TILE, TILE), :] = picked
-        into = s.arrived.at[core, span(me * half, half)]
-        for j in range(share):
-            owner = tile * share + j
-            block = s.leaving.at[span(owner * half, half)]
-
-            @pl.when(owner != me)
-            def _():
-                send(block, into, s.land_sent.at[owner], s.land_came.at[me], (owner, core))
-
-            @pl.when(owner == me)
-            def _():
-                s.arrived[core, span(me * half, half), :] = picked[j * half : (j + 1) * half]
-
-    over(tiles, give_rows)
-    for c in range(3):
-        late.source[c * width : (c + 1) * width, :] = matmul(s.normed_t[...], s.d_triple[c]).astype(LOWF)
-    pos_at = 3 * width
+        ship(tile, picked, s.landed, s.land_sent, s.land_came)
+
     pos_half = places // 2
-    hot = one_hot(tile_iota((pos_half, slots), 0) + core * pos_half == s.place_row[...])
-    late.source[pos_at : pos_at + pos_half, :] = matmul(hot, s.d_rows[:slots, :]).astype(LOWF)
-    if pos_at + pos_half < late.source.shape[0]:
-        late.source[pos_at + pos_half :, :] = jnp.zeros(
-            (late.source.shape[0] - pos_at - pos_half, width), LOWF
-        )
-    late.start()
-    swapped(17, s.few_in)
-    s.few_all[me] = s.few[...] + s.few_in[...]
-
-    def give_few(k):
-        where = (me + k + 1) % groups
-        send(s.few_all.at[me], s.few_all.at[me], s.few_sent.at[where], s.few_came.at[me], (where, core))
-
-    over(groups - 1, give_few)
-    early.forward()
-    late.across()
+
+    def give_late():
+        hot = one_hot(tile_iota((pos_half, slots), 0) + core * pos_half == s.place_row[...])
+        late.fill((matmul(hot, s.d_rows[:slots, :]),), 3 * width)
+
     swapped(1, s.reqs.at[other])
     s.grad_table[...] = jnp.zeros(s.grad_table.shape, WIDE)
 
-    def gather(side, group):
-        came = s.arrived[side, span(group * GROUP, GROUP), :]
+    def gather(side, spot):
+        came = pair_of(s.landed, side, spot)
         first_row = core * held + 1
-        lines = [s.reqs[side, pl.ds(2 * group + i, 1), :] - first_row for i in range(2)]
-
+        lines = [s.reqs[side, pl.ds(spot + b * bank, 1), :] - first_row for b in range(2)]
         rows = tile_iota((held, TILE), 0)
         hot = jnp.concatenate([one_hot(rows == line) for line in lines], 1)
         s.grad_table[...] += matmul(hot, came)
 
-    def between(k):
-        @pl.when(k == 1)
-        def _():
-            late.settle()
-
-        @pl.when(k == 4)
-        def _():
-            late.forward()
-
-    take_all(s.arrived, s.land_came, s.hand_sent, s.hand_came, gather, between)
+    def between(h):
+        first, last = range(late.rounds - 1), range(late.rounds - 1, late.rounds)
+        back, end = range(late.rounds - 1, 0, -1), range(1)
+        plan = {
+            0: (give_late,),
+            1: (lambda: early.settle(first),),
+            2: (lambda: early.settle(last),),
+            3: (late.across, lambda: early.forward(back)),
+            4: (lambda: early.forward(end), lambda: late.settle(first)),
+            5: (lambda: late.settle(last),),
+            6: (lambda: late.forward(back),),
+            7: (lambda: late.forward(end),),
+        }
+        for at, acts in plan.items():
+            for act in acts:
+                pl.when(h == at)(act)
+
+    trade(3, give_rows, s.landed, s.land_came, s.hand_sent, s.hand_came, gather, between)
     final = s.grad_table[...]
     table_ref[...] = final
-    square = (
-        jnp.sum(final * final)
-        + jnp.sum(early.shard[...] * early.shard[...])
-        + jnp.sum(late.shard[...] * late.shard[...])
-    )
-    s.squares[slot_of] = jnp.full((8, TILE), square, WIDE)
-
-    def square_copy(k):
-        where = (slot_of + k + 1) % (2 * groups)
-        block = s.squares.at[slot_of]
-        return copy_to(
-            block, block, s.square_sent.at[where], s.square_came.at[slot_of], (where // 2, where % 2)
-        )
-
-    over(2 * groups - 1, lambda k: square_copy(k).start())
+    square = jnp.sum(final * final)
+    for part in sums:
+        square = square + jnp.sum(part.shard[...] * part.shard[...])
+    s.few[5:6, :] = jnp.full((1, width), square, WIDE)
+    swap(17, s.few, s.few_in)
+    swapped(17, s.few_in)
+    s.few_all[me] = s.few[...] + s.few_in[...]
+
+    def few_copy(k):
+        where = (me + k + 1) % groups
+        block = s.few_all.at[me]
+        return copy_to(block, block, s.few_sent.at[where], s.few_came.at[me], (where, core))
+
+    over(groups - 1, lambda k: few_copy(k).start())
     late.collect()
-    position_own = s.late_whole.at[pos_at : pos_at + pos_half]
+    position_own = late.whole.at[pl.ds(3 * width, pos_half)]
     swap(18, position_own, s.other_half)
     early.collect()
-    early_ref[...] = s.early_whole[: early_ref.shape[0], :]
-    late_ref[...] = s.late_whole[: late_ref.shape[0], :]
+    mid_ref[...] = early.whole[: mid_ref.shape[0], :]
+    down_ref[...] = early.whole[mid_ref.shape[0] : mid_ref.shape[0] + hidden, :]
+    inward_ref[...] = late.whole[: 3 * width, :]
+    position_ref[span(core * pos_half, pos_half), :] = late.whole[3 * width : 3 * width + pos_half, :]
+    swapped(18, s.other_half)
+    position_ref[span(other * pos_half, pos_half), :] = s.other_half[...]
 
     def take_few(k):
         where = (me + k + 1) % groups
@@ -959,38 +994,23 @@
     for source in range(1, groups):
         few_total = few_total + s.few_all[source]
     few_ref[...] = few_total
-    position_ref[span(core * pos_half, pos_half), :] = s.late_whole[pos_at : pos_at + pos_half, :]
-    swapped(18, s.other_half)
-    position_ref[span(other * pos_half, pos_half), :] = s.other_half[...]
-
-    def take_square(k):
-        where = (slot_of + k + 1) % (2 * groups)
-        arrived(s.squares.at[where], s.square_came.at[where])
-
-    over(2 * groups - 1, take_square)
     gains = few_total[:3]
-    norm = jnp.sqrt(jnp.sum(s.squares[...], 0) + jnp.sum(gains * gains))
-    stats_ref[...] = norm
+    stats_ref[...] = jnp.sqrt(few_total[5:6, :TILE] + jnp.sum(gains * gains)) + jnp.zeros((8, TILE), WIDE)
 
     for copy in keep:
         copy.wait()
-    early.drain()
-    late.drain()
+    for part in sums:
+        part.drain()
 
     def finish(k):
         where = (me + k + 1) % groups
         departed(s.want.at[where], s.want_sent.at[where])
-        departed(s.leaving.at[span(where * half, half)], s.land_sent.at[where])
-        departed(s.few_all.at[me], s.few_sent.at[where])
+        departed(s.leaving.at[seat(where)], s.land_sent.at[where])
 
     over(groups - 1, finish)
 
-    def finish_group(group):
-        block = s.arrived.at[core, span(group * GROUP, GROUP)]
-        departed(block, s.hand_sent.at[group])
-
-    over(spans, finish_group)
-    over(2 * groups - 1, lambda k: square_copy(k).wait_send())
+    over(bank, lambda spot: departed(s.landed.at[core, :, spot], s.hand_sent.at[spot]))
+    over(groups - 1, lambda k: few_copy(k).wait_send())
     ends = [s.table.at[rows_mine], s.reqs.at[core], s.w_out.at[core], s.w_up.at[core], s.w_down.at[core]]
     ends += [s.cands.at[mine], s.normed.at[mine]]
     ends += [s.mixed.at[hp, yours] for hp in range(2)] + [s.d_heads_out.at[hp] for hp in range(2)]
@@ -1017,18 +1037,19 @@
         functools.partial(step_kernel, groups, keeps, tuple(scratch)),
         out_shape=(
             shape((held, width), WIDE),
-            shape((heads_width + 2 * hidden, width), LOWF),
-            shape((3 * heads_width, width), LOWF),
+            shape((hidden, width), LOWF),
+            shape((heads_width + hidden, width), LOWF),
+            shape((3 * width, width), LOWF),
             shape((places, width), LOWF),
             shape((8, width), WIDE),
             shape((8, TILE), WIDE),
             *(shape(array.shape, WIDE) for array in kept),
         ),
         in_specs=[VMEM] * 3 + [SMEM] + [VMEM] * 2 + [FAR] * len(arrays),
-        out_specs=(VMEM,) * (6 + len(kept)),
+        out_specs=(VMEM,) * (7 + len(kept)),
         scratch_shapes=list(scratch.values()),
         compiler_params=pltpu.CompilerParams(
-            collective_id=0, has_side_effects=True, vmem_limit_bytes=(48 if keeps else 60) * 1024 * 1024
+            collective_id=0, has_side_effects=True, vmem_limit_bytes=(50 if keeps else 60) * 1024 * 1024
         ),
     )(owners, offsets, seg, live, logq, gains, *(in_hbm(array) for array in arrays))
 
@@ -1040,7 +1061,7 @@
     return (weight - rate * (moved + decay * weight), first, second)
 
 
-def update_kernel(kept, table_g, early_g, late_g, position_g, few_ref, stats_ref, *refs):
+def update_kernel(kept, table_g, down_g, mid_g, inward_g, position_g, few_ref, stats_ref, *refs):
     inputs, outputs, buffers = refs[:21], refs[21:45], refs[45:63]
     came, left = refs[63], refs[64]
     names = ("table", "in", "out", "up", "down", "position")
@@ -1061,18 +1082,18 @@
     outputs[22][0, 0] = few_ref[4, 0]
     outputs[23][0, 0] = norm
     width = table_g.shape[1]
-    block = 16
     for index, name in enumerate(names):
         trio = buffers[3 * index : 3 * index + 3]
         sources = inputs[3 * index : 3 * index + 3] if kept else trio
         for copy in ins[3 * index : 3 * index + 3]:
             copy.wait()
         rate = RATE_POSITION if name == "position" else RATE
+        block = {"table": 112, "up": 32}.get(name, 64)
         lead = trio[0].shape[0] if name == "in" else 1
         rows, columns = trio[0].shape[-2:]
         heads_width, hidden = buffers[6].shape[0], buffers[9].shape[1]
 
-        def run(r, name=name, trio=trio, sources=sources, rows=rows, rate=rate):
+        def run(r, block=block, name=name, trio=trio, sources=sources, rows=rows, rate=rate):
             at = span(r * block, block)
 
             def view(ref):
@@ -1082,19 +1103,19 @@
             if name == "table":
                 grad = table_g[at, :]
             elif name == "in":
-                grad = late_g[at, :].astype(WIDE)
+                grad = inward_g[at, :].astype(WIDE)
             elif name == "out":
-                grad = early_g[at, :].astype(WIDE)
+                grad = mid_g[at, :].astype(WIDE)
             elif name == "up":
                 grad = jnp.concatenate(
                     [
-                        early_g[span(heads_width + c * width + r * block, block), :].astype(WIDE)
+                        mid_g[span(heads_width + c * width + r * block, block), :].astype(WIDE)
                         for c in range(hidden // width)
                     ],
                     1,
                 )
             elif name == "down":
-                grad = early_g[span(heads_width + hidden + r * block, block), :].astype(WIDE)
+                grad = down_g[at, :].astype(WIDE)
             else:
                 grad = position_g[at, :].astype(WIDE)
             made = adamw(values[0], grad * factor, values[1], values[2], DECAY, rate)
@@ -1116,7 +1137,7 @@
     return pl.pallas_call(
         functools.partial(update_kernel, bool(kept)),
         out_shape=tuple(shape(a.shape, WIDE) for a in flat) + (scalar,) * 3,
-        in_specs=[VMEM] * 6 + [VMEM if kept else FAR] * 18 + [VMEM] * 3,
+        in_specs=[VMEM] * 7 + [VMEM if kept else FAR] * 18 + [VMEM] * 3,
         out_specs=(FAR,) * 18 + (VMEM,) * 3 + (SMEM,) * 3,
         scratch_shapes=[pltpu.VMEM(a.shape, WIDE) for a in flat[:18]] + [DMA((18,)), DMA((18,))],
         compiler_params=pltpu.CompilerParams(vmem_limit_bytes=(24 if kept else 48) * 1024 * 1024),
@@ -1161,7 +1182,7 @@
         (norm_gains, gains_first, gains_second),
     )
     groups = lax.axis_size("dp")
-    grads = run_step(
+    made = run_step(
         trios[:6],
         owner_group.reshape(1, -1),
         row_offset,
@@ -1172,7 +1193,7 @@
         groups,
         groups <= 16,
     )
-    made = run_update(grads[:6], trios, grads[6:])
+    made = run_update(made[:7], trios, made[7:])
     return (*made[:21], *(scalar.reshape(()) for scalar in made[21:]))
 
 

time: 136 us -> 125 us (0.919)
  Pallas kernels: 134 us -> 123 us
    pallas_call x1, Pallas kernels: 126 us -> 117 us  [run_step(): pl.pallas_call(functools.partial(step_kernel, groups, keeps, tuple(scratc...]
    pallas_call x1, Pallas kernels: 8.04 us -> 5.71 us  [run_update(): pl.pallas_call(functools.partial(update_kernel, bool(kept)), out_shape=tu...]
where the time goes in v3:
time: 125 us
  Pallas kernels  123 us (98%)
  between operations  1.51 us (1%)
    pallas_call x1, Pallas kernels, run_step(): pl.pallas_call(functools.partial(step_kernel, groups, keeps, tuple(scratc...  117 us
    pallas_call x1, Pallas kernels, run_update(): pl.pallas_call(functools.partial(update_kernel, bool(kept)), out_shape=tu...  5.71 us

profile of v3, /device:TPU:0, one launch (start us, length us, event | category | flops | bytes accessed | tf_op | source)
XLA Modules:
  0.0 124.9 jit_solution(8449152023385417442)
XLA Ops:
  1.3 117.0 %shard_map.433 = (f32[784,256]{1,0:T(8,128)S(1)}, bf16[512,256]{1,0:T(8,128)(2,1)S(1)}, bf16[768,256]{1,0:T(8,128)(2,1)S(1)}, bf16[768,256]{1,0:T(8,128)(2,1)S(1...) custom-call(s32[1,2048]{1,0:T(1,128)} %bitcast.4, ...), custom_call_target="tpu_custom_call" | custom-call | tf_op jit(solution)/shard_map/pallas_call | solution.py:1036
  118.3 0.0 copy-start.2
  118.3 0.0 copy-start.1
  118.3 0.0 copy-start
  118.3 0.7 copy-done.2
  119.0 0.0 copy-done.1
  119.0 0.0 copy-done
  119.0 5.7 %shard_map.434 = (f32[784,256]{1,0:T(8,128)}, f32[784,256]{1,0:T(8,128)}, f32[784,256]{1,0:T(8,128)}, f32[3,256,256]{2,1,0:T(8,128)}, f32[3,256,256]{2,1,0:T(8,1...) custom-call(f32[784,256]{1,0:T(8,128)S(1)} %get-tuple-element.73.tab, ...), custom_call_target="tpu_custom_call" | custom-call | tf_op jit(solution)/shard_map/pallas_call | solution.py:1137
Async XLA Ops:
  118.3 0.7 copy-start.2
  118.3 0.7 copy-start.1
  118.3 0.7 copy-start

commit v4 on v3

--- a/solution.py
+++ b/solution.py
@@ -945,19 +945,18 @@
         back, end = range(late.rounds - 1, 0, -1), range(1)
         plan = {
             0: (give_late,),
-            1: (lambda: early.settle(first),),
-            2: (lambda: early.settle(last),),
-            3: (late.across, lambda: early.forward(back)),
-            4: (lambda: early.forward(end), lambda: late.settle(first)),
-            5: (lambda: late.settle(last),),
-            6: (lambda: late.forward(back),),
-            7: (lambda: late.forward(end),),
+            3: (lambda: early.settle(first),),
+            4: (lambda: early.settle(last), late.across),
+            5: (lambda: early.forward(back), lambda: late.settle(first)),
+            6: (lambda: early.forward(end), lambda: late.settle(last)),
+            7: (lambda: late.forward(back),),
+            8: (lambda: late.forward(end),),
         }
         for at, acts in plan.items():
             for act in acts:
                 pl.when(h == at)(act)
 
-    trade(3, give_rows, s.landed, s.land_came, s.hand_sent, s.hand_came, gather, between)
+    trade(2, give_rows, s.landed, s.land_came, s.hand_sent, s.hand_came, gather, between)
     final = s.grad_table[...]
     table_ref[...] = final
     square = jnp.sum(final * final)
@@ -985,6 +984,27 @@
     swapped(18, s.other_half)
     position_ref[span(other * pos_half, pos_half), :] = s.other_half[...]
 
+    for copy in keep:
+        copy.wait()
+    for part in sums:
+        part.drain()
+
+    def finish(k):
+        where = (me + k + 1) % groups
+        departed(s.want.at[where], s.want_sent.at[where])
+        departed(s.leaving.at[seat(where)], s.land_sent.at[where])
+
+    over(groups - 1, finish)
+
+    over(bank, lambda spot: departed(s.landed.at[core, :, spot], s.hand_sent.at[spot]))
+    ends = [s.table.at[rows_mine], s.reqs.at[core], s.w_out.at[core], s.w_up.at[core], s.w_down.at[core]]
+    ends += [s.cands.at[mine], s.normed.at[mine]]
+    ends += [s.mixed.at[hp, yours] for hp in range(2)] + [s.d_heads_out.at[hp] for hp in range(2)]
+    ends += [s.g_down_out, s.g_up_out, s.g_out_out, s.d_cand, s.d_normed.at[yours]]
+    ends += [s.d_rows.at[mine], s.few]
+    for index, ref in enumerate(ends):
+        departed(ref, s.sent.at[index])
+
     def take_few(k):
         where = (me + k + 1) % groups
         arrived(s.few_all.at[where], s.few_came.at[where])
@@ -996,28 +1016,8 @@
     few_ref[...] = few_total
     gains = few_total[:3]
     stats_ref[...] = jnp.sqrt(few_total[5:6, :TILE] + jnp.sum(gains * gains)) + jnp.zeros((8, TILE), WIDE)
-
-    for copy in keep:
-        copy.wait()
-    for part in sums:
-        part.drain()
-
-    def finish(k):
-        where = (me + k + 1) % groups
-        departed(s.want.at[where], s.want_sent.at[where])
-        departed(s.leaving.at[seat(where)], s.land_sent.at[where])
-
-    over(groups - 1, finish)
-
-    over(bank, lambda spot: departed(s.landed.at[core, :, spot], s.hand_sent.at[spot]))
     over(groups - 1, lambda k: few_copy(k).wait_send())
-    ends = [s.table.at[rows_mine], s.reqs.at[core], s.w_out.at[core], s.w_up.at[core], s.w_down.at[core]]
-    ends += [s.cands.at[mine], s.normed.at[mine]]
-    ends += [s.mixed.at[hp, yours] for hp in range(2)] + [s.d_heads_out.at[hp] for hp in range(2)]
-    ends += [s.g_down_out, s.g_up_out, s.g_out_out, s.d_cand, s.d_normed.at[yours]]
-    ends += [s.d_rows.at[mine], s.few, position_own]
-    for index, ref in enumerate(ends):
-        departed(ref, s.sent.at[index])
+    departed(position_own, s.sent.at[18])
 
 
 def in_hbm(array):
@@ -1057,27 +1057,24 @@
 def adamw(weight, grad, first, second, decay, rate):
     first = BETA_ONE * first + (1.0 - BETA_ONE) * grad
     second = BETA_TWO * second + (1.0 - BETA_TWO) * grad * grad
-    moved = first / (1.0 - BETA_ONE**STEP) / (jnp.sqrt(second / (1.0 - BETA_TWO**STEP)) + ADAM_EPS)
-    return (weight - rate * (moved + decay * weight), first, second)
+    below = jnp.sqrt(second) + ADAM_EPS * (1.0 - BETA_TWO**STEP) ** 0.5
+    pace = rate * (1.0 - BETA_TWO**STEP) ** 0.5 / (1.0 - BETA_ONE**STEP)
+    return ((1.0 - rate * decay) * weight - pace * (first / below), first, second)
 
 
 def update_kernel(kept, table_g, down_g, mid_g, inward_g, position_g, few_ref, stats_ref, *refs):
-    inputs, outputs, buffers = refs[:21], refs[21:45], refs[45:63]
-    came, left = refs[63], refs[64]
+    inputs, outputs, buffers, trio_gains = refs[:21], refs[21:45], refs[45:63], refs[63:66]
+    came, left, gains_came = refs[66:69]
     names = ("table", "in", "out", "up", "down", "position")
     ins = []
     if not kept:
         ins = [pltpu.make_async_copy(inputs[i], buffers[i], came.at[i]) for i in range(18)]
     outs = [pltpu.make_async_copy(buffers[i], outputs[i], left.at[i]) for i in range(18)]
-    for copy in ins:
+    gains_in = [pltpu.make_async_copy(inputs[18 + i], trio_gains[i], gains_came.at[i]) for i in range(3)]
+    for copy in ins + gains_in:
         copy.start()
     norm = stats_ref[0, 0]
     factor = CLIP / jnp.maximum(norm, CLIP)
-    gains = adamw(
-        inputs[18][...], few_ref[0:3, :] * factor, inputs[19][...], inputs[20][...], 0.0, RATE_GAINS
-    )
-    for ref, value in zip(outputs[18:21], gains):
-        ref[...] = value
     outputs[21][0, 0] = few_ref[3, 0]
     outputs[22][0, 0] = few_ref[4, 0]
     outputs[23][0, 0] = norm
@@ -1125,21 +1122,33 @@
         over(lead * rows // block, run)
         for i in range(3):
             outs[3 * index + i].start()
+    for copy in gains_in:
+        copy.wait()
+    gains = adamw(
+        trio_gains[0][...],
+        few_ref[0:3, :] * factor,
+        trio_gains[1][...],
+        trio_gains[2][...],
+        0.0,
+        RATE_GAINS,
+    )
+    for ref, value in zip(outputs[18:21], gains):
+        ref[...] = value
     for copy in outs:
         copy.wait()
 
 
 def run_update(grads, trios, kept):
     flat = [*kept] if kept else [in_hbm(array) for trio in trios[:6] for array in trio]
-    flat += trios[6]
+    flat += [in_hbm(array) for array in trios[6]]
     shape = jax.ShapeDtypeStruct
     scalar = shape((1, 1), WIDE)
     return pl.pallas_call(
         functools.partial(update_kernel, bool(kept)),
         out_shape=tuple(shape(a.shape, WIDE) for a in flat) + (scalar,) * 3,
-        in_specs=[VMEM] * 7 + [VMEM if kept else FAR] * 18 + [VMEM] * 3,
+        in_specs=[VMEM] * 7 + [VMEM if kept else FAR] * 18 + [FAR] * 3,
         out_specs=(FAR,) * 18 + (VMEM,) * 3 + (SMEM,) * 3,
-        scratch_shapes=[pltpu.VMEM(a.shape, WIDE) for a in flat[:18]] + [DMA((18,)), DMA((18,))],
+        scratch_shapes=[pltpu.VMEM(a.shape, WIDE) for a in flat] + [DMA((18,)), DMA((18,)), DMA((3,))],
         compiler_params=pltpu.CompilerParams(vmem_limit_bytes=(24 if kept else 48) * 1024 * 1024),
     )(*grads, *flat)
 

time: 125 us -> 123 us (0.984)
  Pallas kernels: 123 us -> 121 us
    pallas_call x1, Pallas kernels: 117 us -> 115 us  [run_step(): pl.pallas_call(functools.partial(step_kernel, groups, keeps, tuple(scratc...]
where the time goes in v4:
time: 123 us; the launch traced here: 122 us
  Pallas kernels  121 us (98%)
  between operations  1.48 us (1%)
    pallas_call x1, Pallas kernels, run_step(): pl.pallas_call(functools.partial(step_kernel, groups, keeps, tuple(scratc...  115 us
    pallas_call x1, Pallas kernels, run_update(): pl.pallas_call(functools.partial(update_kernel, bool(kept)), out_shape=tu...  5.64 us

profile of v4, /device:TPU:0, one launch (start us, length us, event | category | flops | bytes accessed | tf_op | source)
XLA Modules:
  0.0 122.1 jit_solution(4135925522351298927)
XLA Ops:
  1.3 115.0 %shard_map.433 = (f32[784,256]{1,0:T(8,128)S(1)}, bf16[512,256]{1,0:T(8,128)(2,1)S(1)}, bf16[768,256]{1,0:T(8,128)(2,1)S(1)}, bf16[768,256]{1,0:T(8,128)(2,1)S(1...) custom-call(s32[1,2048]{1,0:T(1,128)} %bitcast.4, ...), custom_call_target="tpu_custom_call" | custom-call | tf_op jit(solution)/shard_map/pallas_call | solution.py:1036
  116.3 5.6 %shard_map.434 = (f32[784,256]{1,0:T(8,128)}, f32[784,256]{1,0:T(8,128)}, f32[784,256]{1,0:T(8,128)}, f32[3,256,256]{2,1,0:T(8,128)}, f32[3,256,256]{2,1,0:T(8,1...) custom-call(f32[784,256]{1,0:T(8,128)S(1)} %get-tuple-element.73.tab, ...), custom_call_target="tpu_custom_call" | custom-call | tf_op jit(solution)/shard_map/pallas_call | solution.py:1146

commit v5 on v4

--- a/solution.py
+++ b/solution.py
@@ -804,7 +804,8 @@
         s.d_third[at, :] = d_third
         s.d_branch[at, :] = d_third.astype(LOWF)
 
-    over(own // TILE, choose)
+    for r in range(own // TILE):
+        choose(jnp.int32(r))
     s.g_down_out[...] = matmul(s.hidden[other], s.d_branch[...], TN).astype(LOWF)
     swap(11, s.g_down_out, s.g_down_in)
     d_cand = matmul(s.d_logits[...], s.final[...], TN)

time: 123 us -> 122 us (level)
  Pallas kernels: 121 us -> 119 us
    pallas_call x1, Pallas kernels: 115 us -> 114 us  [run_step(): pl.pallas_call(functools.partial(step_kernel, groups, keeps, tuple(scratc...]
where the time goes in v5:
time: 122 us; the launch traced here: 121 us
  Pallas kernels  119 us (98%)
  between operations  1.48 us (1%)
    pallas_call x1, Pallas kernels, run_step(): pl.pallas_call(functools.partial(step_kernel, groups, keeps, tuple(scratc...  114 us
    pallas_call x1, Pallas kernels, run_update(): pl.pallas_call(functools.partial(update_kernel, bool(kept)), out_shape=tu...  5.64 us

profile of v5, /device:TPU:0, one launch (start us, length us, event | category | flops | bytes accessed | tf_op | source)
XLA Modules:
  0.0 120.7 jit_solution(1976762687234585243)
XLA Ops:
  1.3 113.6 %shard_map.433 = (f32[784,256]{1,0:T(8,128)S(1)}, bf16[512,256]{1,0:T(8,128)(2,1)S(1)}, bf16[768,256]{1,0:T(8,128)(2,1)S(1)}, bf16[768,256]{1,0:T(8,128)(2,1)S(1...) custom-call(s32[1,2048]{1,0:T(1,128)} %bitcast.4, ...), custom_call_target="tpu_custom_call" | custom-call | tf_op jit(solution)/shard_map/pallas_call | solution.py:1037
  114.9 5.6 %shard_map.434 = (f32[784,256]{1,0:T(8,128)}, f32[784,256]{1,0:T(8,128)}, f32[784,256]{1,0:T(8,128)}, f32[3,256,256]{2,1,0:T(8,128)}, f32[3,256,256]{2,1,0:T(8,1...) custom-call(f32[784,256]{1,0:T(8,128)S(1)} %get-tuple-element.73.tab, ...), custom_call_target="tpu_custom_call" | custom-call | tf_op jit(solution)/shard_map/pallas_call | solution.py:1147
